TPU v7x, 128 devices: a whole 4x4x4 slice. The times are simulated.
128 devices in a mesh: dp: 32 (over x_hi, z, y), seq: 4 (over x_lo, core).
Axes of the slice: x: 4 (x_hi: 2, x_lo: 2; x = x_hi * 2 + x_lo), y: 4, z: 4, core: 2. Of those that a mesh axis runs over, the one named last changes fastest.
Arguments:
- inputs: bfloat16 [32, 2048, 1536], P('dp', 'seq'), may hold values from -6 to 6
- cotangent: bfloat16 [32, 2048, 1536], P('dp', 'seq'), may hold values from -6 to 6
- conv_weight: float32 [768, 5, 768], P('dp'), may hold values from -0.09375 to 0.09375
- query_weight: float32 [1536, 512], P('dp'), as said below
- key_weight: float32 [1536, 128], P('dp'), as said below
- value_weight: float32 [1536, 128], P('dp'), may hold values from -0.15625 to 0.15625
- output_weight: float32 [512, 1536], P('dp'), may hold values from -0.25 to 0.25
- conv_gain: float32 [768], P('dp'), may hold values from 0.5 to 1.5
- attention_gain: float32 [1536], P('dp'), may hold values from 0.5 to 1.5
Outputs:
- input_grad: bfloat16 [32, 2048, 1536], P('dp', 'seq')
- conv_grad: float32 [768, 5, 768], P('dp')
- query_grad: float32 [1536, 512], P('dp')
- key_grad: float32 [1536, 128], P('dp')
- value_grad: float32 [1536, 128], P('dp')
- output_grad: float32 [512, 1536], P('dp')
- convnorm_grad: float32 [768], P('dp')
- attnnorm_grad: float32 [1536], P('dp')
Inputs may be any that keep to these rules, and one draw needn't show every extreme that they name: `query_weight`: a projection scaled by its fan-in, to which some heads may add a component along the key projection of up to about 30 times the key projection's size, so that scores can reach several hundred. `key_weight`: a projection scaled by its fan-in.
All inputs are finite; a program needn't handle non-finite values.
Results may differ from a plain program's by a relative error of at most 0.035.
The roundings to bfloat16 on the way count: a program that leaves them out, or rounds other values in their place, can miss the bound.
Values may be sent and summed in bfloat16 or wider, within the bound.
No kernel may reach another device: no remote copies, remote signals or barrier semaphores. Data moves between devices by JAX's collectives and lax.ppermute only.
A program may use at most 192 MiB of HBM per device.

v0:
```python
import jax
import jax.numpy as jnp
from jax import lax
from jax.experimental import pallas as pl
from jax.experimental.pallas import tpu as pltpu
from jax.sharding import Mesh
from jax.sharding import PartitionSpec as P

EPS = 1e-05
ROOT_HALF = 0.7071067811865476
INV_ROOT_TWO_PI = 0.3989422804014327
LOG2_E = 1.4426950408889634
AXES = ("xh", "z", "y", "xl", "core")
DP = ("xh", "z", "y")
SEQ = ("xl", "core")
F32 = jnp.float32
BF16 = jnp.bfloat16


def gelu_value(before):
    return before * 0.5 * (1.0 + lax.erf(before * ROOT_HALF))


def gelu_slope(before):
    cumulative = 0.5 * (1.0 + lax.erf(before * ROOT_HALF))
    return cumulative + before * INV_ROOT_TWO_PI * jnp.exp(-0.5 * before * before)


def rms_parts(stream):
    inverse = lax.rsqrt(jnp.mean(stream * stream, axis=-1, keepdims=True) + EPS)
    return (inverse, stream * inverse)


def rotate(block, axis, step):
    return lax.ppermute(block, axis, [(i, (i + step) % 4) for i in range(4)])


def swap(block, axis):
    return lax.ppermute(block, axis, [(0, 1), (1, 0)])


def swap_both(block, axes):
    return lax.ppermute(block, axes, [(i, 3 - i) for i in range(4)])


def piece(array, at, dim):
    return lax.dynamic_index_in_dim(array, lax.rem(at, 4), dim, keepdims=False)


def scatter_ring(block, axis, dim):
    place = lax.axis_index(axis)
    total = piece(block, place, dim).astype(F32)
    for step in (2, 1, 3):
        total = total + rotate(piece(block, place + step, dim), axis, step).astype(F32)
    return total.astype(BF16)


def sum_four(block, axis):
    total = block
    for step in (1, 3, 2):
        total = total + rotate(block, axis, step)
    return total


def after(array, *others):
    for other in others:
        array = array + (other.reshape(-1)[0] * 0).astype(array.dtype)
    return array


def pick(flag, first, second):
    return jnp.where(flag == 0, first, second)


def attention_kernel(
    q_ref, k_ref, v_ref, g_ref, o_ref, dq_ref, dk_ref, dv_ref, dk_sum, dv_sum, k_turned, v_turned
):
    step = pl.program_id(0)
    scale = 128 ** (-0.5)

    @pl.when(step == 0)
    def _():
        k_turned[...] = k_ref[...].T
        v_turned[...] = v_ref[...].T

    q = q_ref[...]
    g = g_ref[...]
    nt = (((1,), (1,)), ((), ()))
    scores = lax.dot_general(k_ref[...], q, nt, preferred_element_type=F32)
    top = jnp.max(scores, axis=0, keepdims=True)
    raised = jnp.exp2((scores - top) * (scale * LOG2_E))
    probs = raised * (1.0 / jnp.sum(raised, axis=0, keepdims=True))
    probs_low = probs.astype(BF16)
    o_ref[...] = jnp.dot(v_turned[...], probs_low, preferred_element_type=F32).T.astype(BF16)
    dv = jnp.dot(probs_low, g, preferred_element_type=F32)
    dp = lax.dot_general(v_ref[...], g, nt, preferred_element_type=F32)
    centre = jnp.sum(probs * dp, axis=0, keepdims=True)
    ds = (probs * ((dp - centre) * scale)).astype(BF16)
    dq_ref[...] = jnp.dot(k_turned[...], ds, preferred_element_type=F32).T.astype(BF16)
    dk = jnp.dot(ds, q, preferred_element_type=F32)

    @pl.when(step == 0)
    def _():
        dk_sum[...] = dk
        dv_sum[...] = dv

    @pl.when(step > 0)
    def _():
        dk_sum[...] += dk
        dv_sum[...] += dv

    @pl.when(step == pl.num_programs(0) - 1)
    def _():
        dk_ref[...] = dk_sum[...].astype(BF16)
        dv_ref[...] = dv_sum[...].astype(BF16)


def attention(queries, keys, values, grads, rows=256):
    length, wide = queries.shape
    total, size = keys.shape
    blocks = length // rows
    steps = blocks * (wide // size)
    row_spec = pl.BlockSpec((rows, size), lambda i: (i % blocks, i // blocks))
    full_spec = pl.BlockSpec((total, size), lambda i: (0, 0))
    return pl.pallas_call(
        attention_kernel,
        grid=(steps,),
        in_specs=[row_spec, full_spec, full_spec, row_spec],
        out_specs=[row_spec, row_spec, full_spec, full_spec],
        out_shape=[
            jax.ShapeDtypeStruct((length, wide), BF16),
            jax.ShapeDtypeStruct((length, wide), BF16),
            jax.ShapeDtypeStruct((total, size), BF16),
            jax.ShapeDtypeStruct((total, size), BF16),
        ],
        scratch_shapes=[pltpu.VMEM((total, size), F32)] * 2 + [pltpu.VMEM((size, total), BF16)] * 2,
        compiler_params=pltpu.CompilerParams(
            dimension_semantics=("arbitrary",), vmem_limit_bytes=48 * 1024 * 1024
        ),
        cost_estimate=pl.CostEstimate(
            flops=10 * length * wide * total, bytes_accessed=8 * length * wide, transcendentals=0
        ),
        name="attention",
    )(queries, keys, values, grads)


def prepare_kernel(
    place_ref, own_ref, partner_ref, edge_ref, spare_ref, hidden_ref, gain_ref, wide
):
    core, xl = place_ref[0], place_ref[1]
    channels = hidden_ref.shape[1]
    length = own_ref.shape[0]
    gains = spare_ref[...].astype(F32).T[:8]
    gain_ref[...] = gains
    gain = gains[:1]

    def rows_of(rows):
        _, normed = rms_parts(rows.astype(F32))
        return gelu_value(normed[:, :channels] * gain)

    chunk = 128

    def body(i, carry):
        at = pl.multiple_of(i * chunk, chunk)
        wide[pl.ds(pl.multiple_of(8 + core * length + at, 8), chunk)] = rows_of(
            own_ref[pl.ds(at, chunk)]
        )
        wide[pl.ds(pl.multiple_of(8 + (1 - core) * length + at, 8), chunk)] = rows_of(
            partner_ref[pl.ds(at, chunk)]
        )
        return carry

    lax.fori_loop(0, length // chunk, body, 0)
    edge = rows_of(edge_ref[...])
    reach = edge.shape[0]
    wide[8 - reach : 8] = jnp.where(xl == 1, edge, 0.0)
    end = 8 + 2 * length
    wide[end : end + 16] = jnp.zeros((16, channels), F32)
    wide[end : end + reach] = jnp.where(xl == 0, edge, 0.0)
    for i in range(2 * length // chunk):
        start = 8 - reach + i * chunk
        hidden_ref[i * chunk : (i + 1) * chunk] = wide[start : start + chunk].astype(BF16)
    start = end - reach
    hidden_ref[2 * length : 2 * length + 16] = wide[start : start + 16].astype(BF16)


def prepare(place, own, partner, edge, weights):
    length = own.shape[0]
    channels, wide = weights.shape
    vmem = pl.BlockSpec(memory_space=pltpu.VMEM)
    return pl.pallas_call(
        prepare_kernel,
        grid=(1,),
        in_specs=[
            pl.BlockSpec(memory_space=pltpu.SMEM), vmem, vmem, vmem,
            pl.BlockSpec((channels, 128), lambda i: (0, wide // 128 - 1)),
        ],
        out_specs=[vmem, vmem],
        out_shape=[
            jax.ShapeDtypeStruct((2 * length + 16, channels), BF16),
            jax.ShapeDtypeStruct((8, channels), F32),
        ],
        scratch_shapes=[pltpu.VMEM((2 * length + 32, channels), F32)],
        compiler_params=pltpu.CompilerParams(vmem_limit_bytes=40 * 1024 * 1024),
        name="prepare",
    )(place, own, partner, edge, weights)


def input_kernel(
    core_ref,
    keep_ref,
    away_ref,
    before_ref,
    after_ref,
    weight_ref,
    other_ref,
    middle_ref,
    stream_ref,
    gain_ref,
    out_ref,
    term_ref,
    keep_wide,
    away_wide,
):
    step = pl.program_id(0)
    length, half = keep_ref.shape
    rows, model = stream_ref.shape
    channels = 2 * half
    reach = before_ref.shape[0]
    width = 2 * reach + 1
    second = core_ref[0] == 1

    @pl.when(step == 0)
    def _():
        for wide, rows_ref, flip in ((keep_wide, keep_ref, False), (away_wide, away_ref, True)):
            wide[8 : 8 + length] = rows_ref[...].astype(F32)
            for edge_ref, start in ((before_ref, 8 - reach), (after_ref, 8 + length)):
                edge = edge_ref[...].astype(F32)
                sides = (edge[:, :half], edge[:, half:])
                if flip:
                    sides = sides[::-1]
                wide[start : start + reach] = jnp.where(second, sides[1], sides[0])
        term_ref[...] = jnp.zeros(term_ref.shape, F32)

    at = pl.multiple_of(step * rows, rows)
    hidden_grad = jnp.zeros((rows, channels), F32)
    for wide, weights in ((keep_wide, weight_ref), (away_wide, other_ref)):
        block = wide[pl.ds(at, rows + 16)]
        for offset in range(width):
            start = 8 + reach - offset
            hidden_grad = hidden_grad + lax.dot_general(
                block[start : start + rows].astype(BF16),
                weights[:, offset * half : (offset + 1) * half],
                (((1,), (1,)), ((), ())),
                preferred_element_type=F32,
            )
    stream = stream_ref[...].astype(F32)
    inverse, normed = rms_parts(stream)
    gain = gain_ref[...]
    narrow = normed[:, :channels]
    before_grad = hidden_grad * gelu_slope(narrow * gain)
    term_ref[...] += jnp.sum((before_grad * narrow).reshape(rows // 8, 8, channels), axis=0)
    lifted = before_grad * gain
    projected = jnp.sum(lifted * narrow, axis=-1, keepdims=True) * (1.0 / model)
    out_ref[:, :channels] = (
        middle_ref[:, :channels] + inverse * (lifted - narrow * projected)
    ).astype(BF16)
    out_ref[:, channels:] = (
        middle_ref[:, channels:] - inverse * normed[:, channels:] * projected
    ).astype(BF16)


def input_gradient(core, keep, away, before, behind, weights, other, middle, stream, gain):
    length, model = stream.shape
    half = keep.shape[1]
    rows = 128
    vmem = pl.BlockSpec(memory_space=pltpu.VMEM)
    row_spec = pl.BlockSpec((rows, model), lambda i: (i, 0))
    input_rows, terms = pl.pallas_call(
        input_kernel,
        grid=(length // rows,),
        in_specs=[pl.BlockSpec(memory_space=pltpu.SMEM)]
        + [vmem] * 6
        + [row_spec, row_spec, vmem],
        out_specs=[row_spec, pl.BlockSpec((8, 2 * half), lambda i: (0, 0))],
        out_shape=[
            jax.ShapeDtypeStruct((length, model), BF16),
            jax.ShapeDtypeStruct((8, 2 * half), F32),
        ],
        scratch_shapes=[pltpu.VMEM((length + 16, half), F32)] * 2,
        compiler_params=pltpu.CompilerParams(
            dimension_semantics=("arbitrary",), vmem_limit_bytes=40 * 1024 * 1024
        ),
        cost_estimate=pl.CostEstimate(
            flops=40 * length * half * half, bytes_accessed=16 * length * model, transcendentals=0
        ),
        name="input_gradient",
    )(
        core.reshape(1).astype(jnp.int32), keep, away, before, behind, weights, other, middle,
        stream, gain.reshape(1, -1),
    )
    return input_rows, jnp.sum(terms, axis=0)


def project_kernel(
    core_ref, half_ref, other_ref, own_ref, partner_ref, gain_ref, rest_ref, up_ref,
    attn_ref, query_ref, kv_ref, grad_ref, qkv_ref, out_full,
):
    step = pl.program_id(0)
    rows, half = half_ref.shape
    model = own_ref.shape[1]
    steps = pl.num_programs(0)
    groups = model // 32
    quarter = query_ref.shape[1]
    share = quarter // 16

    @pl.when(step == 0)
    def _():
        for at in range(16):
            for side in range(2):
                start = side * (model // 2) + at * groups
                qkv_ref[start : start + groups] = rest_ref[at, :, side * half : (side + 1) * half]
            third = model // 3
            for part in range(3):
                out_full[at * share : (at + 1) * share, part * third : (part + 1) * third] = rest_ref[
                    at, part * share : (part + 1) * share, 2 * half : 2 * half + third
                ]

    second = core_ref[0] == 1
    mine = half_ref[...].astype(F32)
    other = other_ref[...].astype(F32)
    from_partner = (step >= steps // 2) != second
    at = lax.rem(step, steps // 2) * rows
    at = pl.multiple_of(at, rows)
    outer = jnp.where(
        from_partner,
        partner_ref[pl.ds(at, rows), 2 * half :].astype(F32),
        own_ref[pl.ds(at, rows), 2 * half :].astype(F32),
    )
    middle = jnp.concatenate(
        [jnp.where(second, other, mine), jnp.where(second, mine, other), outer], axis=1
    )
    _, normed = rms_parts(middle)
    attn = (normed * gain_ref[...]).astype(BF16)
    attn_ref[...] = attn
    both = jnp.dot(attn, qkv_ref[...], preferred_element_type=F32).astype(BF16)
    query_ref[...] = both[:, :quarter]
    kv_ref[...] = both[:, quarter:]
    grad_ref[...] = lax.dot_general(
        up_ref[...], out_full[...], (((1,), (1,)), ((), ())), preferred_element_type=F32
    ).astype(BF16)


def project(core, half_rows, other_rows, own, partner, gain, rest, upward, quarter):
    length, half = half_rows.shape
    model = own.shape[1]
    rows = 256
    vmem = pl.BlockSpec(memory_space=pltpu.VMEM)

    def by_rows(wide):
        return pl.BlockSpec((rows, wide), lambda i: (i, 0))

    return pl.pallas_call(
        project_kernel,
        grid=(length // rows,),
        in_specs=[
            pl.BlockSpec(memory_space=pltpu.SMEM), by_rows(half), by_rows(half), vmem, vmem, vmem,
            pl.BlockSpec(rest.shape[:2] + (2 * half + model // 3,), lambda i: (0, 0, 0)),
            by_rows(model),
        ],
        out_specs=[
            by_rows(model), by_rows(quarter), by_rows(half - quarter), by_rows(quarter),
            pl.BlockSpec((model, half), lambda i: (0, 0)),
        ],
        out_shape=[
            jax.ShapeDtypeStruct((length, wide), BF16)
            for wide in (model, quarter, half - quarter, quarter)
        ]
        + [jax.ShapeDtypeStruct((model, half), BF16)],
        scratch_shapes=[pltpu.VMEM((quarter, model), BF16)],
        compiler_params=pltpu.CompilerParams(
            dimension_semantics=("arbitrary",), vmem_limit_bytes=40 * 1024 * 1024
        ),
        cost_estimate=pl.CostEstimate(
            flops=2 * length * model * (half + quarter), bytes_accessed=8 * length * model,
            transcendentals=0,
        ),
        name="project",
    )(
        core.reshape(1).astype(jnp.int32), half_rows, other_rows, own, partner,
        gain.reshape(1, -1), rest, upward,
    )


def projection_kernel(attn_ref, query_ref, attended_ref, upward_ref, out_ref):
    tn = (((0,), (0,)), ((), ()))
    model = attn_ref.shape[1]
    wide = query_ref.shape[1]
    groups = model // 32
    for side in range(2):
        rows = model // 2
        term = lax.dot_general(
            attn_ref[:, side * rows : (side + 1) * rows],
            query_ref[...],
            tn,
            preferred_element_type=F32,
        ).astype(BF16)
        for at in range(16):
            out_ref[at // 4, at % 4, side * groups : (side + 1) * groups] = term[
                at * groups : (at + 1) * groups
            ]
    attended = attended_ref[...]
    share = wide // 16
    for block in range(model // wide):
        term = lax.dot_general(
            attended,
            upward_ref[:, block * wide : (block + 1) * wide],
            tn,
            preferred_element_type=F32,
        ).astype(BF16)
        start = 2 * groups + block * share
        for at in range(16):
            out_ref[at // 4, at % 4, start : start + share] = term[at * share : (at + 1) * share]


def projection_gradient(attn, queries, attended, upward):
    length, model = attn.shape
    wide = queries.shape[1]
    vmem = pl.BlockSpec(memory_space=pltpu.VMEM)
    return pl.pallas_call(
        projection_kernel,
        in_specs=[vmem] * 4,
        out_specs=vmem,
        out_shape=jax.ShapeDtypeStruct((4, 4, model // 8, wide), BF16),
        compiler_params=pltpu.CompilerParams(vmem_limit_bytes=40 * 1024 * 1024),
        cost_estimate=pl.CostEstimate(
            flops=4 * length * model * wide, bytes_accessed=8 * length * model, transcendentals=0
        ),
        name="projection_gradient",
    )(attn, queries, attended, upward)


def on_device(
    inputs,
    cotangent,
    conv_weight,
    query_weight,
    key_weight,
    value_weight,
    output_weight,
    conv_gain,
    attention_gain,
):
    core = lax.axis_index("core")
    xl = lax.axis_index("xl")
    xh = lax.axis_index("xh")
    place = lax.axis_index(DP)
    rows_in, width, channels = conv_weight.shape
    half = channels // 2
    reach = width // 2
    length, model = inputs.shape[1:]
    head_size = key_weight.shape[1]
    query_size = query_weight.shape[1]
    quarter = query_size // 2
    rows_d = query_weight.shape[0]
    rows_o = output_weight.shape[0]
    upward_low = cotangent[0]
    stream_low = inputs[0]
    tn = (((0,), (0,)), ((), ()))
    nt = (((1,), (1,)), ((), ()))

    def both(mine, other):
        return jnp.concatenate([pick(core, mine, other), pick(core, other, mine)], axis=0)

    def own_rows(array):
        return pick(core, array[:length], array[length:])

    def partner_rows(array):
        return pick(core, array[length:], array[:length])

    with jax.named_scope("gather_conv"):
        own = conv_weight.astype(BF16)
        own = pick(core, own[:, :, :half], own[:, :, half:]).reshape(rows_in, width * half)
        gains = jnp.concatenate(
            [
                conv_gain[:, None],
                attention_gain.reshape(rows_in, 2),
                jnp.zeros((rows_in, 125), F32),
            ],
            axis=1,
        )
        own = jnp.concatenate([own, gains.astype(BF16)], axis=1)

    with jax.named_scope("gather"):
        qkv = jnp.concatenate(
            [
                pick(core, query_weight[:, :quarter], query_weight[:, quarter:]),
                pick(core, key_weight, value_weight),
            ],
            axis=1,
        ).astype(BF16)
        third = model // 3
        out_low = jnp.concatenate(
            [output_weight[:, i * third : (i + 1) * third].astype(BF16) for i in range(3)], axis=0
        )
        block = jnp.concatenate(
            [qkv, out_low, jnp.concatenate([own[:, : 2 * third], own[:, 2 * third :]], axis=0)],
            axis=1,
        )
        far = swap(block, "xh")
        pair = [pick(xh, block, far), pick(xh, far, block)]
        start = half + third
        conv_pair = [
            jnp.concatenate(
                [b[:rows_in, start:], b[rows_in:, start:]], axis=1
            )
            for b in pair
        ]
        block = jnp.concatenate(
            [
                pair[0][:, :half],
                pair[1][:, :half],
                pick(xh ^ core, block[:, half:start], far[:, half:start]),
                jnp.concatenate(conv_pair, axis=0),
            ],
            axis=1,
        )
        block = lax.all_gather(block, ("z", "y"), axis=0, tiled=False)
        start = 2 * half + third
        conv_half = block[:, :, start:].reshape(16, 2, rows_in, -1)
        conv_half = conv_half.transpose(1, 0, 2, 3).reshape(channels, -1)

    with jax.named_scope("rows"):
        partner = swap(stream_low, "core")
        edge = after(pick(xl, stream_low[-reach:], stream_low[:reach]), own)
        edge = lax.ppermute(edge, SEQ, [(2, 0), (1, 3)]) + lax.ppermute(edge, SEQ, [(2, 1), (1, 2)])
        upward_pair = both(upward_low, swap(upward_low, "core"))
        inner = both(stream_low[:, :channels], partner[:, :channels])
        inner = pick(core, inner[:, :half], inner[:, half:])

    spots = jnp.stack([core, xl]).astype(jnp.int32)
    hidden, gains = prepare(spots, stream_low, partner, edge, conv_half)
    gain_one = gains[0]
    gain_two = gains[1:3].T.reshape(-1)

    def tap(array, offset):
        return array[:, offset * half : (offset + 1) * half]

    with jax.named_scope("conv"):
        conv_out = jnp.zeros((2 * length, half), F32)
        for offset in range(width):
            conv_out = conv_out + jnp.dot(
                hidden[offset : offset + 2 * length],
                tap(conv_half, offset),
                preferred_element_type=F32,
            )
        middle_half = (inner.astype(F32) + conv_out).astype(BF16)
        middle_other = swap(middle_half, "core")
        middle = jnp.concatenate(
            [
                own_rows(pick(core, middle_half, middle_other)),
                own_rows(pick(core, middle_other, middle_half)),
                stream_low[:, channels:],
            ],
            axis=1,
        )

    attn_pair, queries, kv, attended_grad, qkv_half = project(
        core, middle_half, middle_other, stream_low, partner, gain_two, block, upward_pair, quarter
    )

    with jax.named_scope("keys"):
        kv_far = swap(kv, "xl")
        kv_mine = jnp.concatenate([kv, kv_far], axis=0)
        kv_other = jnp.concatenate([swap(kv, "core"), swap(kv_far, "core")], axis=0)
        keys = pick(core, kv_mine, kv_other)
        values = pick(core, kv_other, kv_mine)

    attended, query_grad_rows, key_part, value_part = attention(
        queries, keys, values, attended_grad
    )

    with jax.named_scope("key_grads"):
        kv_sum = pick(core, key_part, value_part).astype(F32) + swap(
            pick(core, value_part, key_part), "core"
        ).astype(F32)
        kv_sum = kv_sum.astype(BF16)
        kv_grad_low = (
            kv_sum[: 2 * length].astype(F32) + swap(kv_sum[2 * length :], "xl").astype(F32)
        ).astype(BF16)
        query_grad_other = swap(partner_rows(query_grad_rows), "core")
        kv_grad_other = swap(partner_rows(kv_grad_low), "core")

    with jax.named_scope("projection_grads"):
        rest = projection_gradient(attn_pair, query_grad_rows, attended, upward_pair)
        rest_stage = lax.psum_scatter(rest, "z", scatter_dimension=0, tiled=False)
        rest = scatter_ring(rest_stage, "y", 0)
        qkv_other = swap(qkv_half, "core")
        conv_other = swap(conv_half, "core")
        attn_in_grad = lax.dot_general(
            own_rows(query_grad_rows), qkv_half[:, :quarter], nt, preferred_element_type=F32
        )
        attn_in_grad = attn_in_grad + lax.dot_general(
            query_grad_other, qkv_other[:, :quarter], nt, preferred_element_type=F32
        )
        attn_in_grad = attn_in_grad + lax.dot_general(
            own_rows(kv_grad_low), qkv_half[:, quarter:], nt, preferred_element_type=F32
        )
        attn_in_grad = attn_in_grad + lax.dot_general(
            kv_grad_other, qkv_other[:, quarter:], nt, preferred_element_type=F32
        )

    with jax.named_scope("middle_grad"):
        inverse_two, normed_two = rms_parts(middle.astype(F32))
        second_term = jnp.sum(attn_in_grad * normed_two, axis=0)
        scaled_grad = attn_in_grad * gain_two
        middle_grad = upward_low.astype(F32) + inverse_two * (
            scaled_grad - normed_two * jnp.mean(scaled_grad * normed_two, axis=-1, keepdims=True)
        )
        conv_grad_low = middle_grad[:, :channels].astype(BF16)

    with jax.named_scope("conv_grad"):
        cg_keep = pick(core, conv_grad_low[:, :half], conv_grad_low[:, half:])
        cg_away = pick(core, conv_grad_low[:, half:], conv_grad_low[:, :half])
        cg_pair = both(cg_keep, swap(cg_away, "core"))
        before_edge = lax.ppermute(conv_grad_low[-reach:], SEQ, [(0, 1), (1, 2), (2, 3)])
        after_edge = lax.ppermute(conv_grad_low[:reach], SEQ, [(1, 0), (2, 1), (3, 2)])

    with jax.named_scope("key_term"):
        kv_low = lax.dot_general(
            attn_pair, kv_grad_low, tn, preferred_element_type=F32
        ).astype(BF16)
        third = rows_d // 3
        kv_low = kv_low.reshape(2, 4, 4, 3, third, head_size)
        kv_low = jnp.concatenate([kv_low[:, :, :, i] for i in range(3)], axis=-1)
        kv_low = jnp.pad(kv_low, ((0, 0),) * 3 + ((0, rows_in - third), (0, 0)))

    with jax.named_scope("conv_grad"):
        conv_term = [
            lax.dot_general(
                hidden[offset : offset + 2 * length], cg_pair, tn, preferred_element_type=F32
            ).astype(BF16).reshape(2, 4, 4, rows_in, half)
            for offset in range(width)
        ]
        conv_term = jnp.stack(conv_term + [kv_low]).transpose(2, 3, 1, 0, 4, 5)

    with jax.named_scope("reduce_conv"):
        shares = lax.psum_scatter(
            conv_term.reshape(4, 4, -1, half), "z", scatter_dimension=0, tiled=False
        )
        shares = lax.psum_scatter(shares, "y", scatter_dimension=0, tiled=False)
        shares = shares.reshape(2, width + 1, rows_in, half)

    input_rows, first_term = input_gradient(
        core, cg_keep, cg_away, before_edge, after_edge, conv_half, conv_other, middle_grad,
        stream_low, gain_one,
    )

    with jax.named_scope("reduce_gains"):
        terms = jnp.concatenate(
            [first_term.reshape(32, rows_in), second_term.reshape(32, rows_d)], axis=1
        )
        terms = sum_four(terms, "y")
        terms = sum_four(terms, "z")
        terms = lax.dynamic_index_in_dim(terms, place, 0, keepdims=False) + lax.dynamic_index_in_dim(
            swap(terms, "xh"), place, 0, keepdims=False
        )
        terms = terms + swap(terms, "core")
        terms = terms + swap(terms, "xl")

    with jax.named_scope("reduce_conv"):
        total = pick(xh, shares[0], shares[1]).astype(F32)
        total = total + swap(pick(xh, shares[1], shares[0]), "xh").astype(F32)
        total = total.astype(BF16)
        mine = total.astype(F32) + swap(total, "xl").astype(F32)
        other = swap(total, "core").astype(F32) + swap_both(total, SEQ).astype(F32)
        first = pick(core, mine, other)
        second = pick(core, other, mine)
        conv_total = jnp.concatenate([first[:width], second[:width]], axis=2).transpose(1, 0, 2)
        key_total, value_total = [
            jnp.concatenate(
                [
                    side[width, :third, i * head_size : (i + 1) * head_size]
                    for i in range(3)
                ],
                axis=0,
            )
            for side in (first, second)
        ]

    with jax.named_scope("reduce_rest"):
        rest = (rest.astype(F32) + swap(rest, "xl").astype(F32)).astype(BF16)
        rest = (rest.astype(F32) + swap(rest, "xh").astype(F32)).astype(BF16)
        rest = jnp.concatenate(
            [pick(xh, rest[:rows_d], rest[rows_d : 2 * rows_d]), rest[2 * rows_d :]], axis=0
        )
        rest_other = swap(rest, "core")
        first = pick(core, rest, rest_other)
        second = pick(core, rest_other, rest)
        query_total = jnp.concatenate([first[:rows_d], second[:rows_d]], axis=1).astype(F32)
        out_rest = pick(xh, first, second)[rows_d:]
        output_total = jnp.concatenate(
            [out_rest[i * rows_o : (i + 1) * rows_o] for i in range(model // quarter)], axis=1
        ).astype(F32)

    return (
        input_rows[None],
        conv_total,
        query_total,
        key_total,
        value_total,
        output_total,
        terms[:rows_in],
        terms[rows_in:],
    )


def solution(mesh):
    grid = Mesh(mesh.devices.reshape(2, 4, 4, 2, 2), AXES)
    in_specs = (
        P(DP, SEQ, None),
        P(DP, SEQ, None),
        P(DP, None, None),
        P(DP, None),
        P(DP, None),
        P(DP, None),
        P(DP, None),
        P(DP),
        P(DP),
    )
    out_specs = (
        P(DP, SEQ, None),
        P(DP, None, None),
        P(DP, None),
        P(DP, None),
        P(DP, None),
        P(DP, None),
        P(DP),
        P(DP),
    )
    return jax.shard_map(
        on_device, mesh=grid, in_specs=in_specs, out_specs=out_specs, check_vma=False
    )
```

profile of v0, /device:TPU:1, one launch (start us, length us, event | category | flops | bytes accessed | tf_op | source)
XLA Modules:
  0.0 291.0 jit_solution(2672388881280222214)
XLA Ops:
  11.8 3.7 %collective-permute-start.3 = (bf16[48,1920]{1,0:T(8,128)(2,1)S(1)}, bf16[48,1920]{1,0:T(8,128)(2,1)S(1)}, u32[]{:S(2)}, u32[]{:S(2)}) collective-permute-start(bf16[48,1920]{1,0:T(8,128)(2,1)S(1)} %maximum_maximum_fusion.1), channel_id=1, source_target_pairs={{0,64},{64,0},{1,65},{65,1},{2,66},{66,2},{3,67},{67,3},{4,68},{68... | collective-permute-start | bytes 552968 | tf_op jit(solution)/shard_map/gather/ppermute | solution.py:39
  15.4 3.9 %collective-permute-done.3 = bf16[48,1920]{1,0:T(8,128)(2,1)S(1)} collective-permute-done((bf16[48,1920]{1,0:T(8,128)(2,1)S(1)}, bf16[48,1920]{1,0:T(8,128)(2,1)S(1)}, u32[]{:S(2)}, u32[]{:S(2)}) %collective-permute-start.3) | collective-permute-done | bytes 184352 | tf_op jit(solution)/shard_map/gather/ppermute | solution.py:39
  23.3 3.3 %collective-permute-start.2 = (bf16[2,1536]{1,0:T(2,128)(2,1)S(1)}, bf16[2,1536]{1,0:T(2,128)(2,1)S(1)}, u32[]{:S(2)}, u32[]{:S(2)}) collective-permute-start(bf16[2,1536]{1,0:T(2,128)(2,1)S(1)} %fusion.85), channel_id=1, source_target_pairs={{2,1},{1,2},{6,5},{5,6},{10,9},{9,10},{14,13},{13,14},{18,17},{17,... | collective-permute-start | bytes 18440 | tf_op jit(solution)/shard_map/rows/ppermute | solution.py:536
  30.5 49.4 %all-gather.3.cloned.1.call-done = bf16[768,3328]{1,0:T(8,128)(2,1)} async-done(((bf16[48,3328]{1,0:T(8,128)(2,1)}), bf16[768,3328]{1,0:T(8,128)(2,1)}) %all-gather.3.cloned.1.call-update) | async-done | bytes 5111824 | tf_op jit(solution)/shard_map/gather/all_gather | solution.py:528
  79.9 2.3 slice.376
  84.1 2.4 prepare.1
  102.6 7.2 %project.1 = (bf16[1024,1536]{1,0:T(8,128)(2,1)S(1)}, bf16[1024,256]{1,0:T(8,128)(2,1)S(1)}, bf16[1024,128]{1,0:T(8,128)(2,1)S(1)}, bf16[1024,256]{1,0:T(8,128)(2,1)S(1)}, bf16[1536,384]{1,0:T(8,128)(2,1)}) custom-call(s32[1]{0:T(128)} %bitcast.core_ref, bf16[1024,384]{1,0:T(8,128)(2,1)} %add_convert_fusion.half_ref, ...), custom_call_target="tpu_custom_call" | custom-call | flops 2013265920 | bytes 12582912 | tf_op jit(solution)/shard_map/project/pallas_call | solution.py:363
  115.0 2.4 collective-permute-done.6
  120.2 25.2 %attention.1 = (bf16[1024,256]{1,0:T(8,128)(2,1)S(1)}, bf16[1024,256]{1,0:T(8,128)(2,1)S(1)}, bf16[2048,128]{1,0:T(8,128)(2,1)S(1)}, bf16[2048,128]{1,0:T(8,128)(2,1)S(1)}) custom-call(bf16[1024,256]{1,0:T(8,128)(2,1)S(1)} %get-tuple-element.23.q_ref, bf16[2048,128]{1,0:T(8,128)(2,1)S(1)} %get-tuple-element.53.k_ref, ...), custom_call_target="tpu_custom_call" | custom-call | flops 5368709120 | bytes 2097152 | tf_op jit(solution)/shard_map/attention/pallas_call | solution.py:125
  155.7 4.7 %collective-permute-done.12 = bf16[1024,128]{1,0:T(8,128)(2,1)S(1)} collective-permute-done((bf16[1024,128]{1,0:T(8,128)(2,1)S(1)}, bf16[1024,128]{1,0:T(8,128)(2,1)S(1)}, u32[]{:S(2)}, u32[]{:S(2)}) %collective-permute-start.12) | collective-permute-done | bytes 262176 | tf_op jit(solution)/shard_map/key_grads/ppermute | solution.py:39
  166.1 3.5 %fusion.9 = (f32[1536]{0:T(1024)}, f32[512]{0:T(512)S(1)}, f32[512,1536]{1,0:T(8,128)S(1)}) fusion(f32[512]{0:T(512)S(1)} %add_rsqrt_fusion, bf16[512,768]{1,0:T(8,128)(2,1)S(1)} %copy-done.24, bf16[512,384]{1,0:T(8,128)(2,1)S(1)} %get-tuple-element.80, bf16[512,384]{1,0:T(8,128)(2,1)S(1)} %copy-done.27, f32[1536]{0:T(1024)S(1)} %mul.57, ...), kind=kOutput, calls=%fused_computation.12 | convolution fusion | flops 414578688 | bytes 15482881 | tf_op jit(solution)/shard_map/projection_grads/dot_general | solution.py:600
  169.6 2.4 fusion.88
  172.0 9.9 %collective-permute-start.17 = (bf16[512,384]{1,0:T(8,128)(2,1)S(1)}, bf16[512,384]{1,0:T(8,128)(2,1)S(1)}, u32[]{:S(2)}, u32[]{:S(2)}) collective-permute-start(bf16[512,384]{1,0:T(8,128)(2,1)S(1)} %broadcast_select_fusion.11.away_ref), channel_id=1, source_target_pairs={{0,1},{1,0},{2,3},{3,2},{4,5},{5,4},{6,7},{7,6},{8,9},{9,8},{10,11... | collective-permute-start | bytes 1179656 | tf_op jit(solution)/shard_map/conv_grad/ppermute | solution.py:39
  198.4 3.3 %collective-permute-start.14 = (bf16[2,768]{1,0:T(2,128)(2,1)S(1)}, bf16[2,768]{1,0:T(2,128)(2,1)S(1)}, u32[]{:S(2)}, u32[]{:S(2)}) collective-permute-start(bf16[2,768]{1,0:T(2,128)(2,1)S(1)} %get-tuple-element.48), channel_id=1, source_target_pairs={{0,1},{1,2},{2,3},{4,5},{5,6},{6,7},{8,9},{9,10},{10,11},{12,13},{... | collective-permute-start | bytes 9224 | tf_op jit(solution)/shard_map/conv_grad/ppermute | solution.py:626
  208.2 11.2 %input_gradient.1 = (bf16[512,1536]{1,0:T(8,128)(2,1)}, f32[8,768]{1,0:T(8,128)S(1)}) custom-call(s32[1]{0:T(128)} %bitcast.core_ref, bf16[512,384]{1,0:T(8,128)(2,1)S(1)} %get-tuple-element.40.keep_ref, bf16[512,384]{1,0:T(8,128)(2,1)S(1)} %copy-done.18, bf16[2,768]{1,0:T(2,128)(2,1)S(1)} %collective-permute-done.14.before_ref, ...), custom_call_target="tpu_custom_call" | custom-call | flops 3019898880 | bytes 12582912 | tf_op jit(solution)/shard_map/input_gradient/pallas_call | solution.py:279
  221.9 2.8 collective-permute-start.22
  236.6 2.8 collective-permute-start.26
  240.2 2.7 collective-permute-start.34
  243.1 3.3 %collective-permute-start.27 = (bf16[144,256]{1,0:T(8,128)(2,1)S(1)}, bf16[144,256]{1,0:T(8,128)(2,1)S(1)}, u32[]{:S(2)}, u32[]{:S(2)}) collective-permute-start(bf16[144,256]{1,0:T(8,128)(2,1)S(1)} %pad_maximum_fusion.4), channel_id=1, source_target_pairs={{0,1},{1,0},{2,3},{3,2},{4,5},{5,4},{6,7},{7,6},{8,9},{9,8},{10,11... | collective-permute-start | bytes 221192 | tf_op jit(solution)/shard_map/reduce_rest/ppermute | solution.py:39
  252.7 12.9 %reduce-scatter.6.cloned.1.call-done = bf16[1,288,384]{2,1,0:T(8,128)(2,1)} async-done(((bf16[4,288,384]{2,1,0:T(8,128)(2,1)}), bf16[1,288,384]{2,1,0:T(8,128)(2,1)}) %reduce-scatter.6.cloned.1.call-update) | async-done | bytes 221200 | tf_op jit(solution)/shard_map/reduce_conv/reduce_scatter | solution.py:651
  266.6 2.8 collective-permute-start.18
  271.8 4.3 %collective-permute-start.21 = (bf16[6,24,384]{2,1,0:T(8,128)(2,1)S(1)}, bf16[6,24,384]{2,1,0:T(8,128)(2,1)S(1)}, u32[]{:S(2)}, u32[]{:S(2)}) collective-permute-start(bf16[6,24,384]{2,1,0:T(8,128)(2,1)S(1)} %fusion.73), channel_id=1, source_target_pairs={{0,3},{1,2},{2,1},{3,0},{4,7},{5,6},{6,5},{7,4},{8,11},{9,10},{10,... | collective-permute-start | bytes 331784 | tf_op jit(solution)/shard_map/reduce_conv/ppermute | solution.py:43
  277.0 2.8 collective-permute-done.21
  279.8 2.4 collective-permute-done.19
  (258 shorter events, 103.9 us)
Async XLA Ops:
  7.2 72.7 %all-gather.3.cloned.1.call-start = ((), (), s32[]{:S(2)}) async-start(), calls=%async_computation.6 | async-start | bytes 5431296 | tf_op jit(solution)/shard_map/gather/all_gather | solution.py:528
  11.8 7.5 %collective-permute-start.3 = (bf16[48,1920]{1,0:T(8,128)(2,1)S(1)}, bf16[48,1920]{1,0:T(8,128)(2,1)S(1)}, u32[]{:S(2)}, u32[]{:S(2)}) collective-permute-start(bf16[48,1920]{1,0:T(8,128)(2,1)S(1)} %maximum_maximum_fusion.1), channel_id=1, source_target_pairs={{0,64},{64,0},{1,65},{65,1},{2,66},{66,2},{3,67},{67,3},{4,68},{68... | collective-permute-start | bytes 552968 | tf_op jit(solution)/shard_map/gather/ppermute | solution.py:39
  20.2 200.6 %reduce-scatter.8.cloned.1.call-start = ((), (), s32[]{:S(2)}) async-start(), calls=%async_computation.5 | async-start | bytes 1966080 | tf_op jit(solution)/shard_map/projection_grads/reduce_scatter | solution.py:596
  20.3 8.3 %collective-permute-start = (bf16[512,1536]{1,0:T(8,128)(2,1)S(1)}, bf16[512,1536]{1,0:T(8,128)(2,1)S(1)}, u32[]{:S(2)}, u32[]{:S(2)}) collective-permute-start(bf16[512,1536]{1,0:T(8,128)(2,1)S(1)} %bitcast.88), channel_id=1, source_target_pairs={{0,1},{1,0},{2,3},{3,2},{4,5},{5,4},{6,7},{7,6},{8,9},{9,8},{10,11... | collective-permute-start | bytes 4718600 | tf_op jit(solution)/shard_map/rows/ppermute | solution.py:39
  27.8 65.8 %collective-permute-start.5 = (bf16[512,1536]{1,0:T(8,128)(2,1)}, bf16[512,1536]{1,0:T(8,128)(2,1)}, u32[]{:S(2)}, u32[]{:S(2)}) collective-permute-start(bf16[512,1536]{1,0:T(8,128)(2,1)} %bitcast.96), channel_id=1, source_target_pairs={{0,1},{1,0},{2,3},{3,2},{4,5},{5,4},{6,7},{7,6},{8,9},{9,8},{10,11... | collective-permute-start | bytes 4718600 | tf_op jit(solution)/shard_map/rows/ppermute | solution.py:39
  109.9 9.1 %collective-permute-start.7 = (bf16[1024,128]{1,0:T(8,128)(2,1)S(1)}, bf16[1024,128]{1,0:T(8,128)(2,1)S(1)}, u32[]{:S(2)}, u32[]{:S(2)}) collective-permute-start(bf16[1024,128]{1,0:T(8,128)(2,1)S(1)} %get-tuple-element.24), channel_id=1, source_target_pairs={{0,1},{1,0},{2,3},{3,2},{4,5},{5,4},{6,7},{7,6},{8,9},{9,8},{10,11... | collective-permute-start | bytes 786440 | tf_op jit(solution)/shard_map/keys/ppermute | solution.py:39
  109.9 7.5 %collective-permute-start.6 = (bf16[1024,128]{1,0:T(8,128)(2,1)S(1)}, bf16[1024,128]{1,0:T(8,128)(2,1)S(1)}, u32[]{:S(2)}, u32[]{:S(2)}) collective-permute-start(bf16[1024,128]{1,0:T(8,128)(2,1)S(1)} %get-tuple-element.24), channel_id=1, source_target_pairs={{0,2},{2,0},{1,3},{3,1},{4,6},{6,4},{5,7},{7,5},{8,10},{10,8},{9,1... | collective-permute-start | bytes 786440 | tf_op jit(solution)/shard_map/keys/ppermute | solution.py:39
  111.1 42.9 %collective-permute-start.10 = (bf16[1536,384]{1,0:T(8,128)(2,1)}, bf16[1536,384]{1,0:T(8,128)(2,1)}, u32[]{:S(2)}, u32[]{:S(2)}) collective-permute-start(bf16[1536,384]{1,0:T(8,128)(2,1)} %get-tuple-element.27), channel_id=1, source_target_pairs={{0,1},{1,0},{2,3},{3,2},{4,5},{5,4},{6,7},{7,6},{8,9},{9,8},{10,11... | collective-permute-start | bytes 3538952 | tf_op jit(solution)/shard_map/projection_grads/ppermute | solution.py:39
  149.8 93.2 %reduce-scatter.4.cloned.1.call-start = ((), (), s32[]{:S(2)}) async-start(), calls=%async_computation.3 | async-start | bytes 4423680 | tf_op jit(solution)/shard_map/reduce_conv/reduce_scatter | solution.py:648
  152.7 7.8 %collective-permute-start.12 = (bf16[1024,128]{1,0:T(8,128)(2,1)S(1)}, bf16[1024,128]{1,0:T(8,128)(2,1)S(1)}, u32[]{:S(2)}, u32[]{:S(2)}) collective-permute-start(bf16[1024,128]{1,0:T(8,128)(2,1)S(1)} %slice.389), channel_id=1, source_target_pairs={{0,2},{2,0},{1,3},{3,1},{4,6},{6,4},{5,7},{7,5},{8,10},{10,8},{9,1... | collective-permute-start | bytes 786440 | tf_op jit(solution)/shard_map/key_grads/ppermute | solution.py:39
  172.0 11.7 %collective-permute-start.17 = (bf16[512,384]{1,0:T(8,128)(2,1)S(1)}, bf16[512,384]{1,0:T(8,128)(2,1)S(1)}, u32[]{:S(2)}, u32[]{:S(2)}) collective-permute-start(bf16[512,384]{1,0:T(8,128)(2,1)S(1)} %broadcast_select_fusion.11.away_ref), channel_id=1, source_target_pairs={{0,1},{1,0},{2,3},{3,2},{4,5},{5,4},{6,7},{7,6},{8,9},{9,8},{10,11... | collective-permute-start | bytes 1179656 | tf_op jit(solution)/shard_map/conv_grad/ppermute | solution.py:39
  194.5 71.1 %reduce-scatter.6.cloned.1.call-start = ((), (), s32[]{:S(2)}) async-start(), calls=%async_computation.4 | async-start | bytes 1105920 | tf_op jit(solution)/shard_map/reduce_conv/reduce_scatter | solution.py:651
  194.6 9.3 %collective-permute-start.16 = (bf16[768,2048]{1,0:T(8,128)(2,1)S(1)}, bf16[768,2048]{1,0:T(8,128)(2,1)}, u32[]{:S(2)}, u32[]{:S(2)}) collective-permute-start(bf16[768,2048]{1,0:T(8,128)(2,1)S(1)} %bitcast.86), channel_id=1, source_target_pairs={{0,1},{1,0},{2,3},{3,2},{4,5},{5,4},{6,7},{7,6},{8,9},{9,8},{10,11... | collective-permute-start | bytes 9437192 | tf_op jit(solution)/shard_map/projection_grads/ppermute | solution.py:39
  196.1 7.7 %collective-permute-start.15 = (bf16[2,768]{1,0:T(2,128)(2,1)}, bf16[2,768]{1,0:T(2,128)(2,1)S(1)}, u32[]{:S(2)}, u32[]{:S(2)}) collective-permute-start(bf16[2,768]{1,0:T(2,128)(2,1)} %get-tuple-element.47), channel_id=1, source_target_pairs={{1,0},{2,1},{3,2},{5,4},{6,5},{7,6},{9,8},{10,9},{11,10},{13,12},{... | collective-permute-start | bytes 9224 | tf_op jit(solution)/shard_map/conv_grad/ppermute | solution.py:627
  221.9 7.8 %collective-permute-start.22 = (bf16[192,256]{1,0:T(8,128)(2,1)S(1)}, bf16[192,256]{1,0:T(8,128)(2,1)S(1)}, u32[]{:S(2)}, u32[]{:S(2)}) collective-permute-start(bf16[192,256]{1,0:T(8,128)(2,1)S(1)} %get-tuple-element.56), channel_id=1, source_target_pairs={{0,8},{4,12},{8,0},{12,4},{1,9},{5,13},{9,1},{13,5},{2,10},{6,14},... | collective-permute-start | bytes 294920 | tf_op jit(solution)/shard_map/projection_grads/ppermute | solution.py:35
  224.7 5.7 %collective-permute-start.24 = (bf16[192,256]{1,0:T(8,128)(2,1)S(1)}, bf16[192,256]{1,0:T(8,128)(2,1)S(1)}, u32[]{:S(2)}, u32[]{:S(2)}) collective-permute-start(bf16[192,256]{1,0:T(8,128)(2,1)S(1)} %get-tuple-element.57), channel_id=1, source_target_pairs={{0,12},{4,0},{8,4},{12,8},{1,13},{5,1},{9,5},{13,9},{2,14},{6,2},{... | collective-permute-start | bytes 294920 | tf_op jit(solution)/shard_map/projection_grads/ppermute | solution.py:35
  225.6 6.0 %collective-permute-start.23 = (bf16[192,256]{1,0:T(8,128)(2,1)S(1)}, bf16[192,256]{1,0:T(8,128)(2,1)S(1)}, u32[]{:S(2)}, u32[]{:S(2)}) collective-permute-start(bf16[192,256]{1,0:T(8,128)(2,1)S(1)} %get-tuple-element.58), channel_id=1, source_target_pairs={{0,4},{4,8},{8,12},{12,0},{1,5},{5,9},{9,13},{13,1},{2,6},{6,10},{... | collective-permute-start | bytes 294920 | tf_op jit(solution)/shard_map/projection_grads/ppermute | solution.py:35
  226.9 5.7 %collective-permute-start.30 = (f32[32,72]{1,0:T(8,128)S(1)}, f32[32,72]{1,0:T(8,128)S(1)}, u32[]{:S(2)}, u32[]{:S(2)}) collective-permute-start(f32[32,72]{1,0:T(8,128)S(1)} %pad_maximum_fusion.7), channel_id=1, source_target_pairs={{0,8},{4,12},{8,0},{12,4},{1,9},{5,13},{9,1},{13,5},{2,10},{6,14},... | collective-permute-start | bytes 27656 | tf_op jit(solution)/shard_map/reduce_gains/ppermute | solution.py:35
  233.9 5.5 %collective-permute-start.33 = (f32[32,72]{1,0:T(8,128)S(1)}, f32[32,72]{1,0:T(8,128)S(1)}, u32[]{:S(2)}, u32[]{:S(2)}) collective-permute-start(f32[32,72]{1,0:T(8,128)S(1)} %add_add_fusion.1), channel_id=1, source_target_pairs={{0,32},{16,48},{32,0},{48,16},{1,33},{17,49},{33,1},{49,17},{2,34}... | collective-permute-start | bytes 27656 | tf_op jit(solution)/shard_map/reduce_gains/ppermute | solution.py:35
  236.6 6.3 %collective-permute-start.26 = (bf16[192,256]{1,0:T(8,128)(2,1)S(1)}, bf16[192,256]{1,0:T(8,128)(2,1)S(1)}, u32[]{:S(2)}, u32[]{:S(2)}) collective-permute-start(bf16[192,256]{1,0:T(8,128)(2,1)S(1)} %add_convert_fusion.4), channel_id=1, source_target_pairs={{0,64},{64,0},{1,65},{65,1},{2,66},{66,2},{3,67},{67,3},{4,68},{68... | collective-permute-start | bytes 294920 | tf_op jit(solution)/shard_map/reduce_rest/ppermute | solution.py:39
  240.2 6.1 %collective-permute-start.34 = (f32[32,72]{1,0:T(8,128)S(1)}, f32[32,72]{1,0:T(8,128)S(1)}, u32[]{:S(2)}, u32[]{:S(2)}) collective-permute-start(f32[32,72]{1,0:T(8,128)S(1)} %add_add_fusion), channel_id=1, source_target_pairs={{0,64},{64,0},{1,65},{65,1},{2,66},{66,2},{3,67},{67,3},{4,68},{68... | collective-permute-start | bytes 27656 | tf_op jit(solution)/shard_map/reduce_gains/ppermute | solution.py:39
  243.1 9.5 %collective-permute-start.27 = (bf16[144,256]{1,0:T(8,128)(2,1)S(1)}, bf16[144,256]{1,0:T(8,128)(2,1)S(1)}, u32[]{:S(2)}, u32[]{:S(2)}) collective-permute-start(bf16[144,256]{1,0:T(8,128)(2,1)S(1)} %pad_maximum_fusion.4), channel_id=1, source_target_pairs={{0,1},{1,0},{2,3},{3,2},{4,5},{5,4},{6,7},{7,6},{8,9},{9,8},{10,11... | collective-permute-start | bytes 221192 | tf_op jit(solution)/shard_map/reduce_rest/ppermute | solution.py:39
  271.8 7.9 %collective-permute-start.21 = (bf16[6,24,384]{2,1,0:T(8,128)(2,1)S(1)}, bf16[6,24,384]{2,1,0:T(8,128)(2,1)S(1)}, u32[]{:S(2)}, u32[]{:S(2)}) collective-permute-start(bf16[6,24,384]{2,1,0:T(8,128)(2,1)S(1)} %fusion.73), channel_id=1, source_target_pairs={{0,3},{1,2},{2,1},{3,0},{4,7},{5,6},{6,5},{7,4},{8,11},{9,10},{10,... | collective-permute-start | bytes 331784 | tf_op jit(solution)/shard_map/reduce_conv/ppermute | solution.py:43
  276.1 6.0 %collective-permute-start.19 = (bf16[6,24,384]{2,1,0:T(8,128)(2,1)S(1)}, bf16[6,24,384]{2,1,0:T(8,128)(2,1)S(1)}, u32[]{:S(2)}, u32[]{:S(2)}) collective-permute-start(bf16[6,24,384]{2,1,0:T(8,128)(2,1)S(1)} %fusion.73), channel_id=1, source_target_pairs={{0,2},{2,0},{1,3},{3,1},{4,6},{6,4},{5,7},{7,5},{8,10},{10,8},{9,1... | collective-permute-start | bytes 331784 | tf_op jit(solution)/shard_map/reduce_conv/ppermute | solution.py:39
  (52 other events, 265.3 us)
Sparse Core Ops, SparseCore 0:
  20.3 59.5 all-gather.2
  149.9 24.2 reduce-scatter.7
  194.7 40.7 reduce-scatter.3
  243.2 22.4 reduce-scatter.5
where the time goes:
time: 296 us; the launch traced here: 291 us
  waiting for transfers between devices  89.3 us (30%)
  starting transfers between devices  62.9 us (21%)
  Pallas kernels  47.9 us (16%)
  local copies, waits for them, and re-layouts  28.2 us (10%)
  other arithmetic  26.3 us (9%)
  matrix products  20.7 us (7%)
  between operations  15.6 us (5%)
    all_gather x1, waiting for transfers between devices, on_device(): block = lax.all_gather(block, ('z', 'y'), axis=0, tiled=False)  49.4 us
    ppermute x23, starting transfers between devices, swap(): return lax.ppermute(block, axis, [(0, 1), (1, 0)])  38.7 us
    pallas_call x1, Pallas kernels, attention(): pl.pallas_call(attention_kernel, grid=(steps,), in_specs=[row_spec, full_...  25.2 us
    ppermute x23, waiting for transfers between devices, swap(): return lax.ppermute(block, axis, [(0, 1), (1, 0)])  19.5 us
    unnamed x84, local copies, waits for them, and re-layouts  18.8 us
    reduce_scatter x1, waiting for transfers between devices, on_device(): shares = lax.psum_scatter(shares, 'y', scatter_dimension=0, tiled=False)  12.9 us
    pallas_call x1, Pallas kernels, input_gradient(): pl.pallas_call(input_kernel, grid=(length // rows,), in_specs=[pl.BlockSp...  11.2 us
    ppermute x9, starting transfers between devices, rotate(): return lax.ppermute(block, axis, [(i, (i + step) % 4) for i in range(4)])  9.72 us
  transfers between devices with their start and end apart: 41, of which 18 were waited for; matrix products, arithmetic and copies ran while one was open for 18% of the time, Pallas kernels for 14%

commit v1 on v0

v1 whole, which is shorter than its diff:
```python
import jax
import jax.numpy as jnp
from jax import lax
from jax.experimental import pallas as pl
from jax.experimental.pallas import tpu as pltpu
from jax.sharding import Mesh
from jax.sharding import PartitionSpec as P

EPS = 1e-05
ROOT_HALF = 0.7071067811865476
INV_ROOT_TWO_PI = 0.3989422804014327
LOG2_E = 1.4426950408889634
AXES = ("xh", "z", "y", "xl", "core")
DP = ("xh", "z", "y")
SEQ = ("xl", "core")
F32 = jnp.float32
BF16 = jnp.bfloat16


def gelu_value(before):
    return before * 0.5 * (1.0 + lax.erf(before * ROOT_HALF))


def gelu_slope(before):
    cumulative = 0.5 * (1.0 + lax.erf(before * ROOT_HALF))
    return cumulative + before * INV_ROOT_TWO_PI * jnp.exp(-0.5 * before * before)


def rms_parts(stream):
    inverse = lax.rsqrt(jnp.mean(stream * stream, axis=-1, keepdims=True) + EPS)
    return (inverse, stream * inverse)


def rotate(block, axis, step):
    return lax.ppermute(block, axis, [(i, (i + step) % 4) for i in range(4)])


def swap(block, axis):
    return lax.ppermute(block, axis, [(0, 1), (1, 0)])


def swap_both(block, axes):
    return lax.ppermute(block, axes, [(i, 3 - i) for i in range(4)])


def piece(array, at, dim):
    return lax.dynamic_index_in_dim(array, lax.rem(at, 4), dim, keepdims=False)


def scatter_ring(block, axis, dim):
    place = lax.axis_index(axis)
    total = piece(block, place, dim).astype(F32)
    for step in (2, 1, 3):
        total = total + rotate(piece(block, place + step, dim), axis, step).astype(F32)
    return total.astype(BF16)


def sum_four(block, axis):
    total = block
    for step in (1, 3, 2):
        total = total + rotate(block, axis, step)
    return total


def after(array, *others):
    for other in others:
        array = array + (other[(0,) * other.ndim] * 0).astype(array.dtype)
    return array


def pick(flag, first, second):
    return jnp.where(flag == 0, first, second)


def attention_kernel(
    core_ref, q_ref, near_ref, far_ref, near_other_ref, far_other_ref, g_ref,
    o_ref, dq_ref, keep_ref, away_ref,
    k_rows, v_rows, k_turned, v_turned, dk_sum, dv_sum,
):
    step = pl.program_id(0)
    scale = 128 ** (-0.5)
    first = core_ref[0] == 0
    rows = near_ref.shape[0]

    @pl.when(step == 0)
    def _():
        for start, mine_ref, other_ref in (
            (0, near_ref, near_other_ref), (rows, far_ref, far_other_ref)
        ):
            mine = mine_ref[...]
            other = other_ref[...]
            k = jnp.where(first, mine, other)
            v = jnp.where(first, other, mine)
            k_rows[start : start + rows] = k
            v_rows[start : start + rows] = v
            k_turned[:, start : start + rows] = k.T
            v_turned[:, start : start + rows] = v.T

    q = q_ref[...]
    g = g_ref[...]
    nt = (((1,), (1,)), ((), ()))
    scores = lax.dot_general(k_rows[...], q, nt, preferred_element_type=F32)
    top = jnp.max(scores, axis=0, keepdims=True)
    raised = jnp.exp2((scores - top) * (scale * LOG2_E))
    probs = raised * (1.0 / jnp.sum(raised, axis=0, keepdims=True))
    probs_low = probs.astype(BF16)
    o_ref[...] = jnp.dot(v_turned[...], probs_low, preferred_element_type=F32).T.astype(BF16)
    dv = jnp.dot(probs_low, g, preferred_element_type=F32)
    dp = lax.dot_general(v_rows[...], g, nt, preferred_element_type=F32)
    centre = jnp.sum(probs * dp, axis=0, keepdims=True)
    ds = (probs * ((dp - centre) * scale)).astype(BF16)
    dq_ref[...] = jnp.dot(k_turned[...], ds, preferred_element_type=F32).T.astype(BF16)
    dk = jnp.dot(ds, q, preferred_element_type=F32)

    @pl.when(step == 0)
    def _():
        dk_sum[...] = dk
        dv_sum[...] = dv

    @pl.when(step > 0)
    def _():
        dk_sum[...] += dk
        dv_sum[...] += dv

    @pl.when(step == pl.num_programs(0) - 1)
    def _():
        dk = dk_sum[...]
        dv = dv_sum[...]
        keep_ref[...] = jnp.where(first, dk, dv).astype(BF16)
        away_ref[...] = jnp.where(first, dv, dk).astype(BF16)


def attention(core, queries, near, far, near_other, far_other, grads, rows=512):
    length, wide = queries.shape
    half, size = near.shape
    total = 2 * half
    blocks = length // rows
    steps = blocks * (wide // size)
    row_spec = pl.BlockSpec((rows, size), lambda i: (i % blocks, i // blocks))
    full_spec = pl.BlockSpec((half, size), lambda i: (0, 0))
    return pl.pallas_call(
        attention_kernel,
        grid=(steps,),
        in_specs=[pl.BlockSpec(memory_space=pltpu.SMEM), row_spec]
        + [full_spec] * 4
        + [row_spec],
        out_specs=[row_spec] * 2 + [pl.BlockSpec((total, size), lambda i: (0, 0))] * 2,
        out_shape=[jax.ShapeDtypeStruct((length, wide), BF16)] * 2
        + [jax.ShapeDtypeStruct((total, size), BF16)] * 2,
        scratch_shapes=[pltpu.VMEM((total, size), BF16)] * 2
        + [pltpu.VMEM((size, total), BF16)] * 2
        + [pltpu.VMEM((total, size), F32)] * 2,
        compiler_params=pltpu.CompilerParams(
            dimension_semantics=("arbitrary",), vmem_limit_bytes=48 * 1024 * 1024
        ),
        cost_estimate=pl.CostEstimate(
            flops=10 * length * wide * total, bytes_accessed=8 * length * wide, transcendentals=0
        ),
        name="attention",
    )(core, queries, near, far, near_other, far_other, grads)


def prepare_kernel(
    place_ref, own_ref, partner_ref, edge_ref, gain_ref, hidden_ref, wide
):
    core, xl = place_ref[0], place_ref[1]
    channels = hidden_ref.shape[1]
    length = own_ref.shape[0]
    gain = gain_ref[...]

    def rows_of(rows):
        _, normed = rms_parts(rows.astype(F32))
        return gelu_value(normed[:, :channels] * gain)

    chunk = 128

    def body(i, carry):
        at = pl.multiple_of(i * chunk, chunk)
        wide[pl.ds(pl.multiple_of(8 + core * length + at, 8), chunk)] = rows_of(
            own_ref[pl.ds(at, chunk)]
        )
        wide[pl.ds(pl.multiple_of(8 + (1 - core) * length + at, 8), chunk)] = rows_of(
            partner_ref[pl.ds(at, chunk)]
        )
        return carry

    lax.fori_loop(0, length // chunk, body, 0)
    edge = rows_of(edge_ref[...])
    reach = edge.shape[0]
    wide[8 - reach : 8] = jnp.where(xl == 1, edge, 0.0)
    end = 8 + 2 * length
    wide[end : end + 16] = jnp.zeros((16, channels), F32)
    wide[end : end + reach] = jnp.where(xl == 0, edge, 0.0)
    for i in range(2 * length // chunk):
        start = 8 - reach + i * chunk
        hidden_ref[i * chunk : (i + 1) * chunk] = wide[start : start + chunk].astype(BF16)
    start = end - reach
    hidden_ref[2 * length : 2 * length + 16] = wide[start : start + 16].astype(BF16)
    hidden_ref[2 * length + 16 :] = jnp.zeros(
        (hidden_ref.shape[0] - 2 * length - 16, channels), BF16
    )


def prepare(place, own, partner, edge, gain):
    length = own.shape[0]
    channels = gain.shape[0]
    vmem = pl.BlockSpec(memory_space=pltpu.VMEM)
    return pl.pallas_call(
        prepare_kernel,
        in_specs=[pl.BlockSpec(memory_space=pltpu.SMEM)] + [vmem] * 4,
        out_specs=vmem,
        out_shape=jax.ShapeDtypeStruct((2 * length + 128, channels), BF16),
        scratch_shapes=[pltpu.VMEM((2 * length + 32, channels), F32)],
        compiler_params=pltpu.CompilerParams(vmem_limit_bytes=40 * 1024 * 1024),
        name="prepare",
    )(place, own, partner, edge, gain.reshape(1, -1))


def conv_kernel(hidden_ref, block_ref, inner_ref, middle_ref, weight_ref, shifted):
    length, half = inner_ref.shape
    rows = shifted.shape[0]
    channels, wide = weight_ref.shape
    group = channels // 32
    for pair in range(8):
        first = block_ref[2 * pair].astype(F32)
        second = block_ref[2 * pair + 1].astype(F32)
        for side in range(2):
            part = slice(side * group, (side + 1) * group)
            start = side * (channels // 2) + pair * 2 * group
            weight_ref[start : start + 2 * group] = jnp.concatenate(
                [first[part], second[part]], axis=0
            ).astype(BF16)
    hidden = hidden_ref[:rows]
    total = jnp.zeros((length, half), F32)
    for tap in range(wide // half):
        shifted[...] = jnp.dot(
            hidden, weight_ref[:, tap * half : (tap + 1) * half], preferred_element_type=F32
        )
        total = total + shifted[tap : tap + length]
    middle_ref[...] = (inner_ref[...].astype(F32) + total).astype(BF16)


def convolve(hidden, block, inner, taps):
    length, half = inner.shape
    channels = hidden.shape[1]
    vmem = pl.BlockSpec(memory_space=pltpu.VMEM)
    return pl.pallas_call(
        conv_kernel,
        grid=(1,),
        in_specs=[
            vmem,
            pl.BlockSpec(block.shape[:2] + (taps * half,), lambda i: (0, 0, 0)),
            vmem,
        ],
        out_specs=[vmem, vmem],
        out_shape=[
            jax.ShapeDtypeStruct((length, half), BF16),
            jax.ShapeDtypeStruct((channels, taps * half), BF16),
        ],
        scratch_shapes=[pltpu.VMEM((length + 16, half), F32)],
        compiler_params=pltpu.CompilerParams(vmem_limit_bytes=40 * 1024 * 1024),
        cost_estimate=pl.CostEstimate(
            flops=2 * taps * channels * half * length, bytes_accessed=8 * channels * channels,
            transcendentals=0,
        ),
        name="convolve",
    )(hidden, block, inner)


def input_kernel(
    keep_ref,
    away_ref,
    before_ref,
    after_ref,
    weight_ref,
    other_ref,
    middle_ref,
    stream_ref,
    gain_ref,
    out_ref,
    term_ref,
    keep_wide,
    away_wide,
):
    step = pl.program_id(0)
    length, half = keep_ref.shape
    rows, model = stream_ref.shape
    channels = 2 * half
    reach = before_ref.shape[0]
    width = 2 * reach + 1

    @pl.when(step == 0)
    def _():
        for wide, rows_ref, flip in ((keep_wide, keep_ref, False), (away_wide, away_ref, True)):
            wide[8 : 8 + length] = rows_ref[...].astype(F32)
            for edge_ref, start in ((before_ref, 8 - reach), (after_ref, 8 + length)):
                edge = edge_ref[...].astype(F32)
                wide[start : start + reach] = edge[:, :half] if flip else edge[:, half:]
        term_ref[...] = jnp.zeros(term_ref.shape, F32)

    at = pl.multiple_of(step * rows, rows)
    hidden_grad = jnp.zeros((rows, channels), F32)
    for wide, weights in ((keep_wide, weight_ref), (away_wide, other_ref)):
        block = wide[pl.ds(at, rows + 16)]
        for offset in range(width):
            start = 8 + reach - offset
            hidden_grad = hidden_grad + lax.dot_general(
                block[start : start + rows].astype(BF16),
                weights[:, offset * half : (offset + 1) * half],
                (((1,), (1,)), ((), ())),
                preferred_element_type=F32,
            )
    stream = stream_ref[...].astype(F32)
    inverse, normed = rms_parts(stream)
    gain = gain_ref[...]
    narrow = normed[:, :channels]
    before_grad = hidden_grad * gelu_slope(narrow * gain)
    term_ref[...] += jnp.sum((before_grad * narrow).reshape(rows // 8, 8, channels), axis=0)
    lifted = before_grad * gain
    projected = jnp.sum(lifted * narrow, axis=-1, keepdims=True) * (1.0 / model)
    out_ref[:, :channels] = (
        middle_ref[:, :channels] + inverse * (lifted - narrow * projected)
    ).astype(BF16)
    out_ref[:, channels:] = (
        middle_ref[:, channels:] - inverse * normed[:, channels:] * projected
    ).astype(BF16)


def input_gradient(keep, away, before, behind, weights, other, middle, stream, gain):
    length, model = stream.shape
    half = keep.shape[1]
    rows = 128
    vmem = pl.BlockSpec(memory_space=pltpu.VMEM)
    row_spec = pl.BlockSpec((rows, model), lambda i: (i, 0))
    input_rows, terms = pl.pallas_call(
        input_kernel,
        grid=(length // rows,),
        in_specs=[vmem] * 6
        + [row_spec, row_spec, vmem],
        out_specs=[row_spec, pl.BlockSpec((8, 2 * half), lambda i: (0, 0))],
        out_shape=[
            jax.ShapeDtypeStruct((length, model), BF16),
            jax.ShapeDtypeStruct((8, 2 * half), F32),
        ],
        scratch_shapes=[pltpu.VMEM((length + 16, half), F32)] * 2,
        compiler_params=pltpu.CompilerParams(
            dimension_semantics=("arbitrary",), vmem_limit_bytes=40 * 1024 * 1024
        ),
        cost_estimate=pl.CostEstimate(
            flops=40 * length * half * half, bytes_accessed=16 * length * model, transcendentals=0
        ),
        name="input_gradient",
    )(
        keep, away, before, behind, weights, other, middle,
        stream, gain.reshape(1, -1),
    )
    return input_rows, jnp.sum(terms, axis=0)


def project_kernel(
    core_ref, half_ref, other_ref, own_ref, partner_ref, gain_ref, rest_ref, last_ref,
    attn_ref, kv_ref, qkv_ref, out_full,
):
    step = pl.program_id(0)
    rows, half = half_ref.shape
    model = gain_ref.shape[1]
    steps = pl.num_programs(0)
    groups = model // 32
    quarter = half - kv_ref.shape[1]
    share = quarter // 16

    @pl.when(step == 0)
    def _():
        for at in range(16):
            rest = jnp.concatenate([rest_ref[at], last_ref[at]], axis=1)
            for side in range(2):
                start = side * (model // 2) + at * groups
                qkv_ref[start : start + groups] = rest[:, side * half : (side + 1) * half]
            third = model // 3
            for part in range(3):
                out_full[at * share : (at + 1) * share, part * third : (part + 1) * third] = rest[
                    part * share : (part + 1) * share, 2 * half :
                ]

    second = core_ref[0] == 1
    mine = half_ref[...].astype(F32)
    other = other_ref[...].astype(F32)
    outer = jnp.where(step >= steps // 2, partner_ref[...], own_ref[...]).astype(F32)
    middle = jnp.concatenate(
        [jnp.where(second, other, mine), jnp.where(second, mine, other), outer], axis=1
    )
    _, normed = rms_parts(middle)
    attn = (normed * gain_ref[...]).astype(BF16)
    attn_ref[...] = attn
    kv_ref[...] = jnp.dot(attn, qkv_ref[:, quarter:], preferred_element_type=F32).astype(BF16)


def project(core, half_rows, other_rows, own, partner, gain, rest, quarter):
    length, half = half_rows.shape
    model = own.shape[1]
    rows = 256
    vmem = pl.BlockSpec(memory_space=pltpu.VMEM)

    steps = length // rows

    def by_rows(wide):
        return pl.BlockSpec(
            (rows, wide), lambda i, core: (lax.rem(i + core[0] * (steps // 2), steps), 0)
        )

    def whole(first, second):
        return pl.BlockSpec((first, second), lambda i, core: (0, 0))

    outer = model - 2 * half
    part = rest.shape[:2] + (rest.shape[2] // 5,)
    return pl.pallas_call(
        project_kernel,
        grid_spec=pltpu.PrefetchScalarGridSpec(
            num_scalar_prefetch=1,
            grid=(steps,),
            in_specs=[
                by_rows(half), by_rows(half),
                pl.BlockSpec((rows, outer), lambda i, core: (lax.min(i, steps // 2 - 1), 1)),
                pl.BlockSpec((rows, outer), lambda i, core: (lax.max(i - steps // 2, 0), 1)),
                whole(1, model),
                pl.BlockSpec(part, lambda i, core: (0, 0, 3)),
                pl.BlockSpec(part, lambda i, core: (0, 0, 4)),
            ],
            out_specs=[
                by_rows(model), by_rows(half - quarter), whole(model, half), whole(quarter, model)
            ],
        ),
        out_shape=[
            jax.ShapeDtypeStruct((length, model), BF16),
            jax.ShapeDtypeStruct((length, half - quarter), BF16),
            jax.ShapeDtypeStruct((model, half), BF16),
            jax.ShapeDtypeStruct((quarter, model), BF16),
        ],
        compiler_params=pltpu.CompilerParams(
            dimension_semantics=("arbitrary",), vmem_limit_bytes=40 * 1024 * 1024
        ),
        cost_estimate=pl.CostEstimate(
            flops=2 * length * model * (half - quarter), bytes_accessed=8 * length * model,
            transcendentals=0,
        ),
        name="project",
    )(core, half_rows, other_rows, own, partner, gain.reshape(1, -1), rest, rest)


def projection_kernel(
    core_ref, attn_ref, query_ref, attended_ref, upward_ref, partner_ref, hidden_ref,
    out_ref, turned_ref,
):
    tn = (((0,), (0,)), ((), ()))
    model = attn_ref.shape[1]
    wide = query_ref.shape[1]
    half = out_ref.shape[3]
    groups = model // 32
    share = wide // 16
    for side in range(2):
        rows = model // 2
        term = lax.dot_general(
            attn_ref[:, side * rows : (side + 1) * rows],
            query_ref[...],
            tn,
            preferred_element_type=F32,
        ).astype(BF16)
        for at in range(16):
            start = at * groups
            line = jnp.concatenate(
                [term[start + i * share : start + (i + 1) * share] for i in range(3)], axis=1
            )
            for i in range(2):
                start = (2 * side + i) * share
                out_ref[at // 4, at % 4, start : start + share] = line[
                    :, i * half : (i + 1) * half
                ]
    length = upward_ref.shape[0]
    core = core_ref[0]
    own = attended_ref[pl.ds(pl.multiple_of(core * length, length), length)]
    partner = attended_ref[pl.ds(pl.multiple_of((1 - core) * length, length), length)]
    for block in range(model // half):
        columns = slice(block * half, (block + 1) * half)
        term = lax.dot_general(own, upward_ref[:, columns], tn, preferred_element_type=F32)
        term = term + lax.dot_general(
            partner, partner_ref[:, columns], tn, preferred_element_type=F32
        )
        term = term.astype(BF16)
        start = (4 + block) * share
        for at in range(16):
            out_ref[at // 4, at % 4, start : start + share] = term[at * share : (at + 1) * share]
    turned_ref[...] = hidden_ref[...].T


def projection_gradient(core, attn, queries, attended, upward, partner, hidden):
    length, model = attn.shape
    wide = queries.shape[1]
    vmem = pl.BlockSpec(memory_space=pltpu.VMEM)
    return pl.pallas_call(
        projection_kernel,
        in_specs=[pl.BlockSpec(memory_space=pltpu.SMEM)] + [vmem] * 6,
        out_specs=[vmem, vmem],
        out_shape=[
            jax.ShapeDtypeStruct((4, 4, 8 * wide // 16, model // 4), BF16),
            jax.ShapeDtypeStruct(hidden.shape[::-1], BF16),
        ],
        compiler_params=pltpu.CompilerParams(vmem_limit_bytes=48 * 1024 * 1024),
        cost_estimate=pl.CostEstimate(
            flops=1000, bytes_accessed=1000, transcendentals=0
        ),
        name="projection_gradient",
    )(core, attn, queries, attended, upward, partner, hidden)


def middle_kernel(
    core_ref, query_ref, query_other_ref, kv_ref, kv_other_ref, weight_ref, other_ref,
    middle_ref, upward_ref, gain_ref, grad_ref, keep_ref, away_ref, term_ref,
):
    step = pl.program_id(0)
    nt = (((1,), (1,)), ((), ()))
    rows, model = middle_ref.shape
    wide = query_ref.shape[1]
    half = keep_ref.shape[1]
    grad = jnp.zeros((rows, model), F32)
    for q_ref, k_ref, w_ref in (
        (query_ref, kv_ref, weight_ref), (query_other_ref, kv_other_ref, other_ref)
    ):
        grad = grad + lax.dot_general(
            q_ref[...], w_ref[:, :wide], nt, preferred_element_type=F32
        )
        grad = grad + lax.dot_general(
            k_ref[...], w_ref[:, wide:], nt, preferred_element_type=F32
        )
    inverse, normed = rms_parts(middle_ref[...].astype(F32))
    product = grad * normed

    @pl.when(step == 0)
    def _():
        term_ref[...] = jnp.zeros(term_ref.shape, F32)

    term_ref[...] += jnp.sum(product.reshape(rows // 8, 8, model), axis=0)
    gain = gain_ref[...]
    mean = jnp.mean(product * gain, axis=-1, keepdims=True)
    result = upward_ref[...].astype(F32) + inverse * (grad * gain - normed * mean)
    grad_ref[...] = result
    low = result[:, :half].astype(BF16)
    high = result[:, half : 2 * half].astype(BF16)
    second = core_ref[0] == 1
    keep_ref[...] = jnp.where(second, high, low)
    away_ref[...] = jnp.where(second, low, high)


def middle_gradient(
    core, queries, queries_other, kv, kv_other, weights, other, middle, upward, gain
):
    length, model = middle.shape
    half = weights.shape[1]
    rows = 128

    def by_rows(wide):
        return pl.BlockSpec((rows, wide), lambda i: (i, 0))

    vmem = pl.BlockSpec(memory_space=pltpu.VMEM)
    grads, keep, away, terms = pl.pallas_call(
        middle_kernel,
        grid=(length // rows,),
        in_specs=[
            pl.BlockSpec(memory_space=pltpu.SMEM),
            by_rows(queries.shape[1]), by_rows(queries.shape[1]),
            by_rows(kv.shape[1]), by_rows(kv.shape[1]),
            vmem, vmem, by_rows(model), by_rows(model), vmem,
        ],
        out_specs=[
            by_rows(model), by_rows(half), by_rows(half),
            pl.BlockSpec((8, model), lambda i: (0, 0)),
        ],
        out_shape=[
            jax.ShapeDtypeStruct((length, model), F32),
            jax.ShapeDtypeStruct((length, half), BF16),
            jax.ShapeDtypeStruct((length, half), BF16),
            jax.ShapeDtypeStruct((8, model), F32),
        ],
        compiler_params=pltpu.CompilerParams(
            dimension_semantics=("arbitrary",), vmem_limit_bytes=40 * 1024 * 1024
        ),
        cost_estimate=pl.CostEstimate(
            flops=4 * length * model * half, bytes_accessed=12 * length * model, transcendentals=0
        ),
        name="middle_gradient",
    )(
        core, queries, queries_other, kv, kv_other, weights, other, middle, upward,
        gain.reshape(1, -1),
    )
    return grads, keep, away, jnp.sum(terms, axis=0)


def conv_term_kernel(core_ref, turned_ref, keep_ref, sent_ref, kv_ref, out_ref, wide):
    length, half = keep_ref.shape
    span = turned_ref.shape[1]
    taps = out_ref.shape[3] - 1
    group = out_ref.shape[4]
    first = core_ref[0] == 0
    keep = keep_ref[...].astype(F32)
    sent = sent_ref[...].astype(F32)
    wide[:8] = jnp.zeros((8, half), F32)
    wide[8 : 8 + length] = jnp.where(first, keep, sent)
    wide[8 + length : 8 + 2 * length] = jnp.where(first, sent, keep)
    wide[8 + 2 * length :] = jnp.zeros((span - 2 * length, half), F32)
    for tap in range(taps):
        shifted = wide[8 - tap : 8 - tap + span].astype(BF16)
        term = jnp.dot(turned_ref[...], shifted, preferred_element_type=F32)
        for at in range(32):
            out_ref[at // 4 % 4, at % 4, at // 16, tap] = term[
                at * group : (at + 1) * group
            ].astype(BF16)
    for at in range(32):
        out_ref[at // 4 % 4, at % 4, at // 16, taps] = kv_ref[at // 16, at // 4 % 4, at % 4]


def conv_terms(core, turned, keep, sent, kv, taps):
    channels, span = turned.shape
    length, half = keep.shape
    vmem = pl.BlockSpec(memory_space=pltpu.VMEM)
    return pl.pallas_call(
        conv_term_kernel,
        in_specs=[pl.BlockSpec(memory_space=pltpu.SMEM)] + [vmem] * 4,
        out_specs=vmem,
        out_shape=jax.ShapeDtypeStruct((4, 4, 2, taps + 1, channels // 32, half), BF16),
        scratch_shapes=[pltpu.VMEM((span + 8, half), F32)],
        compiler_params=pltpu.CompilerParams(vmem_limit_bytes=40 * 1024 * 1024),
        cost_estimate=pl.CostEstimate(
            flops=2 * taps * channels * half * span, bytes_accessed=4 * channels * span,
            transcendentals=0,
        ),
        name="conv_terms",
    )(core, turned, keep, sent, kv)


def on_device(
    inputs,
    cotangent,
    conv_weight,
    query_weight,
    key_weight,
    value_weight,
    output_weight,
    conv_gain,
    attention_gain,
):
    core = lax.axis_index("core")
    xl = lax.axis_index("xl")
    xh = lax.axis_index("xh")
    place = lax.axis_index(DP)
    rows_in, width, channels = conv_weight.shape
    half = channels // 2
    reach = width // 2
    length, model = inputs.shape[1:]
    head_size = key_weight.shape[1]
    query_size = query_weight.shape[1]
    quarter = query_size // 2
    rows_d = query_weight.shape[0]
    rows_o = output_weight.shape[0]
    upward_low = cotangent[0]
    stream_low = inputs[0]
    tn = (((0,), (0,)), ((), ()))
    nt = (((1,), (1,)), ((), ()))

    def both(mine, other):
        return jnp.concatenate([pick(core, mine, other), pick(core, other, mine)], axis=0)

    def own_rows(array):
        return pick(core, array[:length], array[length:])

    def partner_rows(array):
        return pick(core, array[length:], array[:length])

    with jax.named_scope("gather_conv"):
        own = conv_weight.astype(BF16)
        own = pick(core, own[:, :, :half], own[:, :, half:]).reshape(rows_in, width * half)
        own = jnp.pad(own, ((0, 0), (0, 128)))

    with jax.named_scope("gather"):
        qkv = jnp.concatenate(
            [
                pick(core, query_weight[:, :quarter], query_weight[:, quarter:]),
                pick(core, key_weight, value_weight),
            ],
            axis=1,
        ).astype(BF16)
        third = model // 3
        out_low = jnp.concatenate(
            [output_weight[:, i * third : (i + 1) * third].astype(BF16) for i in range(3)], axis=0
        )
        block = jnp.concatenate(
            [qkv, out_low, jnp.concatenate([own[:, : 2 * third], own[:, 2 * third :]], axis=0)],
            axis=1,
        )
        far = swap(block, "xh")
        pair = [pick(xh, block, far), pick(xh, far, block)]
        start = half + third
        left = width * half - 2 * third
        conv_pair = [
            jnp.concatenate([b[:rows_in, start:], b[rows_in:, start : start + left]], axis=1)
            for b in pair
        ]
        block = jnp.concatenate(
            [
                jnp.concatenate(conv_pair, axis=0),
                pair[0][:, :half],
                pair[1][:, :half],
                pick(xh ^ core, block[:, half:start], far[:, half:start]),
            ],
            axis=1,
        )
        own_block = block
        block = lax.all_gather(block, ("z", "y"), axis=0, tiled=False)

    with jax.named_scope("rows"):
        partner = swap(stream_low, "core")
        edge = after(pick(xl, stream_low[-reach:], stream_low[:reach]), own)
        edge = lax.ppermute(edge, SEQ, [(2, 0), (1, 3)]) + lax.ppermute(edge, SEQ, [(2, 1), (1, 2)])
        upward_partner = swap(upward_low, "core")
        inner = both(stream_low[:, :channels], partner[:, :channels])
        inner = pick(core, inner[:, :half], inner[:, half:])

    core_at = core.reshape(1).astype(jnp.int32)
    spots = jnp.stack([core, xl]).astype(jnp.int32)
    with jax.named_scope("gather_gains"):
        slot = lax.broadcasted_iota(jnp.int32, (32, rows_in + rows_d), 0)
        gains = jnp.concatenate([conv_gain, attention_gain]).astype(BF16)
        gains = after(gains, own_block)
        gains = jnp.where(slot == place, gains[None, :], jnp.zeros((), BF16))
        gains = sum_four(gains, "y")
        gains = sum_four(gains, "z")
        gains = (gains + swap(gains, "xh")).astype(F32)
        gain_one = gains[:, :rows_in].reshape(-1)
        gain_two = gains[:, rows_in:].reshape(-1)
    hidden = prepare(spots, stream_low, partner, edge, gain_one)
    with jax.named_scope("conv"):
        middle_half, conv_half = convolve(hidden, block, inner, width)
        middle_other = swap(middle_half, "core")
        middle = jnp.concatenate(
            [
                own_rows(pick(core, middle_half, middle_other)),
                own_rows(pick(core, middle_other, middle_half)),
                stream_low[:, channels:],
            ],
            axis=1,
        )

    attn_pair, kv, qkv_half, out_half = project(
        core_at, middle_half, middle_other, stream_low, partner, gain_two, block, quarter
    )

    with jax.named_scope("project"):
        queries = jnp.dot(attn_pair, qkv_half[:, :quarter], preferred_element_type=F32).astype(BF16)
        upward_pair = both(upward_low, upward_partner)
        attended_grad = lax.dot_general(
            upward_pair, out_half, nt, preferred_element_type=F32
        ).astype(BF16)

    with jax.named_scope("keys"):
        kv_far = swap(kv, "xl")
        kv_near_other = swap(kv, "core")
        kv_far_other = swap(kv_far, "core")

    attended, query_grad_rows, kv_keep, kv_away = attention(
        core_at, queries, kv, kv_far, kv_near_other, kv_far_other, attended_grad
    )

    with jax.named_scope("key_grads"):
        kv_sum = (kv_keep.astype(F32) + swap(kv_away, "core").astype(F32)).astype(BF16)
        kv_grad_low = (
            kv_sum[: 2 * length].astype(F32) + swap(kv_sum[2 * length :], "xl").astype(F32)
        ).astype(BF16)
        query_grad_other = swap(partner_rows(query_grad_rows), "core")
        kv_grad_other = swap(partner_rows(kv_grad_low), "core")

    with jax.named_scope("projection_grads"):
        qkv_other = swap(qkv_half, "core")
        conv_other = swap(conv_half, "core")
        rest, hidden_turned = projection_gradient(
            after(core_at, kv_sum, conv_other, qkv_other), attn_pair, query_grad_rows, attended, upward_low,
            upward_partner, hidden,
        )
        rest = lax.psum_scatter(rest, "z", scatter_dimension=0, tiled=False)

    middle_grad, cg_keep, cg_away, second_term = middle_gradient(
        core_at, own_rows(query_grad_rows), query_grad_other, own_rows(kv_grad_low), kv_grad_other,
        qkv_half, qkv_other, middle, upward_low, gain_two,
    )

    with jax.named_scope("conv_grad"):
        cg_sent = swap(cg_away, "core")

        def ends(rows):
            return jnp.concatenate([cg_keep[rows], cg_away[rows]], axis=1)

        after_edge = lax.ppermute(ends(slice(0, reach)), SEQ, [(1, 0), (2, 1), (3, 2)])
        before_edge = lax.ppermute(ends(slice(length - reach, length)), SEQ, [(0, 1), (1, 2), (2, 3)])

    with jax.named_scope("key_term"):
        kv_low = lax.dot_general(
            attn_pair, kv_grad_low, tn, preferred_element_type=F32
        ).astype(BF16)
        third = rows_d // 3
        kv_low = kv_low.reshape(2, 4, 4, 3, third, head_size)
        kv_low = jnp.concatenate([kv_low[:, :, :, i] for i in range(3)], axis=-1)
        kv_low = jnp.pad(kv_low, ((0, 0),) * 3 + ((0, rows_in - third), (0, 0)))

    conv_term = conv_terms(core_at, hidden_turned, cg_keep, cg_sent, kv_low, width)

    with jax.named_scope("reduce_conv"):
        shares = lax.psum_scatter(
            conv_term.reshape(4, 4, -1, half), "z", scatter_dimension=0, tiled=False
        )

    input_rows, first_term = input_gradient(
        cg_keep, cg_away, before_edge, after_edge, conv_half, conv_other, middle_grad,
        stream_low, gain_one,
    )

    with jax.named_scope("reduce_gains"):
        terms = jnp.concatenate(
            [first_term.reshape(32, rows_in), second_term.reshape(32, rows_d)], axis=1
        )
        terms = sum_four(terms, "z").reshape(2, 4, 4, rows_in + rows_d)
        terms = lax.dynamic_index_in_dim(terms, lax.axis_index("z"), 1, keepdims=False)
        terms = terms.transpose(1, 0, 2)[:, :, None].astype(BF16)
        terms = jnp.pad(terms, ((0, 0), (0, 0), (0, 7), (0, half - rows_in - rows_d)))
        terms = terms.reshape(4, 16, half)

    with jax.named_scope("reduce_all"):
        rest = scatter_ring(rest, "y", 0)
        everything = scatter_ring(jnp.concatenate([shares, terms], axis=1), "y", 0)
        conv_both = 2 * (width + 1) * rows_in
        everything = jnp.concatenate(
            [everything[:conv_both], rest, everything[conv_both:]], axis=0
        )
        conv_rows = (width + 1) * rows_in
        query_rows = rows_d * quarter // half
        out_rows = rows_o * model // half
        sides = []
        start = 0
        for rows in (conv_rows, query_rows, out_rows, 8):
            if rows == out_rows:
                sides.append((everything[start : start + rows],) * 2)
                start += rows
            else:
                sides.append(
                    (everything[start : start + rows], everything[start + rows : start + 2 * rows])
                )
                start += 2 * rows
        keep = jnp.concatenate([pick(xh, a, b) for a, b in sides], axis=0)
        send = jnp.concatenate([pick(xh, b, a) for a, b in sides], axis=0)
        total = (keep.astype(F32) + swap(send, "xh").astype(F32)).astype(BF16)
        mine = total.astype(F32) + swap(total, "xl").astype(F32)
        other = swap(total, "core").astype(F32) + swap_both(total, SEQ).astype(F32)
        first = pick(core, mine, other)
        second = pick(core, other, mine)

        def conv_of(side):
            return side[: width * rows_in].reshape(width, rows_in, half)

        conv_total = jnp.concatenate([conv_of(first), conv_of(second)], axis=2).transpose(1, 0, 2)
        start = width * rows_in
        key_total, value_total = [
            jnp.concatenate(
                [
                    side[start : start + third, i * head_size : (i + 1) * head_size]
                    for i in range(3)
                ],
                axis=0,
            )
            for side in (first, second)
        ]

        def query_of(side):
            line = jnp.concatenate(
                [side[conv_rows : conv_rows + rows_o], side[conv_rows + rows_o : conv_rows + query_rows]],
                axis=1,
            )
            return jnp.concatenate(
                [line[:, i * quarter : (i + 1) * quarter] for i in range(3)], axis=0
            )

        query_total = jnp.concatenate([query_of(first), query_of(second)], axis=1)
        start = conv_rows + query_rows
        out_total = pick(xh, first, second)[start : start + out_rows]
        output_total = jnp.concatenate(
            [out_total[i * rows_o : (i + 1) * rows_o] for i in range(model // half)], axis=1
        )
        terms = (first + second)[start + out_rows, : rows_in + rows_d]

    return (
        input_rows[None],
        conv_total,
        query_total,
        key_total,
        value_total,
        output_total,
        terms[:rows_in],
        terms[rows_in:],
    )


def solution(mesh):
    grid = Mesh(mesh.devices.reshape(2, 4, 4, 2, 2), AXES)
    in_specs = (
        P(DP, SEQ, None),
        P(DP, SEQ, None),
        P(DP, None, None),
        P(DP, None),
        P(DP, None),
        P(DP, None),
        P(DP, None),
        P(DP),
        P(DP),
    )
    out_specs = (
        P(DP, SEQ, None),
        P(DP, None, None),
        P(DP, None),
        P(DP, None),
        P(DP, None),
        P(DP, None),
        P(DP),
        P(DP),
    )
    return jax.shard_map(
        on_device, mesh=grid, in_specs=in_specs, out_specs=out_specs, check_vma=False
    )
```

time: 296 us -> 275 us (0.929)
  waiting for transfers between devices: 89.3 us -> 71.1 us
  Pallas kernels: 47.9 us -> 65.8 us
  matrix products: 20.7 us -> 3.01 us
  starting transfers between devices: 62.9 us -> 71.1 us
  local copies, waits for them, and re-layouts: 28.2 us -> 20.2 us
  other arithmetic: 26.3 us -> 21.5 us
    all_gather x1, waiting for transfers between devices: 49.4 us -> 22.9 us  [on_device(): block = lax.all_gather(block, ('z', 'y'), axis=0, tiled=False)]
    pallas_call x5 -> x8, Pallas kernels: 47.9 us -> 65.8 us  [the longest x1 22.9 us: attention(): pl.pallas_call(attention_kernel, grid=(steps,), in_specs=[pl.BlockSpec(me...]
    dot_general x14 -> x2, matrix products: 19.6 us -> 1.98 us  [the longest x1 1 us: on_device(): lax.dot_general(upward_pair, out_half, nt, preferred_element_type=F32)]
    ppermute x9 -> x15, starting transfers between devices: 9.72 us -> 24.8 us  [rotate(): return lax.ppermute(block, axis, [(i, (i + step) % 4) for i in range(4)])]
    reduce_scatter x2 -> x1, waiting for transfers between devices: 13 us -> 0.02 us  [on_device(): rest = lax.psum_scatter(rest, 'z', scatter_dimension=0, tiled=False)]
    ppermute x9 -> x15, waiting for transfers between devices: 3.96 us -> 11.6 us  [rotate(): return lax.ppermute(block, axis, [(i, (i + step) % 4) for i in range(4)])]
    ppermute x23 -> x18, starting transfers between devices: 38.7 us -> 32.6 us  [swap(): return lax.ppermute(block, axis, [(0, 1), (1, 0)])]
    reduce_scatter x1, waiting for transfers between devices: 0.02 us -> 5.6 us  [on_device(): lax.psum_scatter(conv_term.reshape(4, 4, -1, half), 'z', scatter_dimensio...]
  transfers between devices with their start and end apart: 41 -> 41, of which waited for: 18 -> 19; matrix products, arithmetic and copies ran while one was open for 18% -> 7% of each run, Pallas kernels for 14% -> 22%
where the time goes in v1:
time: 275 us; the launch traced here: 271 us
  starting transfers between devices  71.1 us (26%)
  waiting for transfers between devices  71.1 us (26%)
  Pallas kernels  65.8 us (24%)
  other arithmetic  21.5 us (8%)
  local copies, waits for them, and re-layouts  20.2 us (7%)
  between operations  18.1 us (7%)
  matrix products  3.01 us (1%)
    ppermute x18, starting transfers between devices, swap(): return lax.ppermute(block, axis, [(0, 1), (1, 0)])  32.6 us
    ppermute x15, starting transfers between devices, rotate(): return lax.ppermute(block, axis, [(i, (i + step) % 4) for i in range(4)])  24.8 us
    ppermute x18, waiting for transfers between devices, swap(): return lax.ppermute(block, axis, [(0, 1), (1, 0)])  24.6 us
    pallas_call x1, Pallas kernels, attention(): pl.pallas_call(attention_kernel, grid=(steps,), in_specs=[pl.BlockSpec(me...  22.9 us
    all_gather x1, waiting for transfers between devices, on_device(): block = lax.all_gather(block, ('z', 'y'), axis=0, tiled=False)  22.9 us
    unnamed x65, local copies, waits for them, and re-layouts  14.1 us
    pallas_call x1, Pallas kernels, input_gradient(): pl.pallas_call(input_kernel, grid=(length // rows,), in_specs=[vmem] * 6...  11.9 us
    ppermute x15, waiting for transfers between devices, rotate(): return lax.ppermute(block, axis, [(i, (i + step) % 4) for i in range(4)])  11.6 us
  transfers between devices with their start and end apart: 41, of which 19 were waited for; matrix products, arithmetic and copies ran while one was open for 7% of the time, Pallas kernels for 22%

profile of v1, /device:TPU:1, one launch (start us, length us, event | category | flops | bytes accessed | tf_op | source)
XLA Modules:
  0.0 270.8 jit_solution(5799034316828266823)
XLA Ops:
  11.0 3.6 %collective-permute-start.3 = (bf16[48,1920]{1,0:T(8,128)(2,1)}, bf16[48,1920]{1,0:T(8,128)(2,1)}, u32[]{:S(2)}, u32[]{:S(2)}) collective-permute-start(bf16[48,1920]{1,0:T(8,128)(2,1)} %maximum_maximum_fusion), channel_id=1, source_target_pairs={{0,64},{64,0},{1,65},{65,1},{2,66},{66,2},{3,67},{67,3},{4,68},{68... | collective-permute-start | bytes 552968 | tf_op jit(solution)/shard_map/gather/ppermute | solution.py:39
  14.6 4.2 %collective-permute-done.3 = bf16[48,1920]{1,0:T(8,128)(2,1)} collective-permute-done((bf16[48,1920]{1,0:T(8,128)(2,1)}, bf16[48,1920]{1,0:T(8,128)(2,1)}, u32[]{:S(2)}, u32[]{:S(2)}) %collective-permute-start.3) | collective-permute-done | bytes 184352 | tf_op jit(solution)/shard_map/gather/ppermute | solution.py:39
  38.2 3.1 %collective-permute-start.1 = (bf16[2,1536]{1,0:T(2,128)(2,1)S(1)}, bf16[2,1536]{1,0:T(2,128)(2,1)S(1)}, u32[]{:S(2)}, u32[]{:S(2)}) collective-permute-start(bf16[2,1536]{1,0:T(2,128)(2,1)S(1)} %fusion.43), channel_id=1, source_target_pairs={{2,0},{1,3},{6,4},{5,7},{10,8},{9,11},{14,12},{13,15},{18,16},{17,... | collective-permute-start | bytes 18440 | tf_op jit(solution)/shard_map/rows/ppermute | solution.py:721
  41.3 4.8 %collective-permute-start.2 = (bf16[2,1536]{1,0:T(2,128)(2,1)S(1)}, bf16[2,1536]{1,0:T(2,128)(2,1)S(1)}, u32[]{:S(2)}, u32[]{:S(2)}) collective-permute-start(bf16[2,1536]{1,0:T(2,128)(2,1)S(1)} %fusion.43), channel_id=1, source_target_pairs={{2,1},{1,2},{6,5},{5,6},{10,9},{9,10},{14,13},{13,14},{18,17},{17,... | collective-permute-start | bytes 18440 | tf_op jit(solution)/shard_map/rows/ppermute | solution.py:721
  46.1 2.8 %collective-permute-start.10 = (bf16[32,72]{1,0:T(8,128)(2,1)S(1)}, bf16[32,72]{1,0:T(8,128)(2,1)S(1)}, u32[]{:S(2)}, u32[]{:S(2)}) collective-permute-start(bf16[32,72]{1,0:T(8,128)(2,1)S(1)} %add_add_fusion.1), channel_id=1, source_target_pairs={{0,64},{64,0},{1,65},{65,1},{2,66},{66,2},{3,67},{67,3},{4,68},{68... | collective-permute-start | bytes 13832 | tf_op jit(solution)/shard_map/gather_gains/ppermute | solution.py:39
  50.3 3.2 %prepare.1.hidden_ref = bf16[1152,768]{1,0:T(8,128)(2,1)S(1)} custom-call(s32[2]{0:T(128)S(1)} %pad_add_fusion.place_ref, bf16[512,1536]{1,0:T(8,128)(2,1)S(1)} %bitcast.80, bf16[512,1536]{1,0:T(8,128)(2,1)} %collective-permute-done.partner_ref, bf16[2,1536]{1,0:T(2,128)(2,1)S(1)} %add.168.edge_ref, f32[1,768]{1,0:T(1,128)S(1)} %reshape.110.gain_ref), custom_call_target="tpu_custom_call" | custom-call | tf_op jit(solution)/shard_map/prepare/pallas_call | solution.py:208
  57.4 22.9 %all-gather.3.cloned.1.call-done = bf16[768,3200]{1,0:T(8,128)(2,1)} async-done(((bf16[48,3200]{1,0:T(8,128)(2,1)}), bf16[768,3200]{1,0:T(8,128)(2,1)}) %all-gather.3.cloned.1.call-update) | async-done | bytes 4915216 | tf_op jit(solution)/shard_map/gather/all_gather | solution.py:716
  85.3 6.0 %convolve.1 = (bf16[1024,384]{1,0:T(8,128)(2,1)}, bf16[768,1920]{1,0:T(8,128)(2,1)}) custom-call(bf16[1152,768]{1,0:T(8,128)(2,1)S(1)} %copy-done.6, bf16[16,48,3200]{2,1,0:T(8,128)(2,1)S(1)} %bitcast.86, bf16[1024,384]{1,0:T(8,128)(2,1)S(1)} %copy-done.17), custom_call_target="tpu_custom_call" | custom-call | flops 3019898880 | bytes 4718592 | tf_op jit(solution)/shard_map/conv/convolve/pallas_call | solution.py:247
  94.2 5.1 %project.1 = (bf16[1024,1536]{1,0:T(8,128)(2,1)S(1)}, bf16[1024,128]{1,0:T(8,128)(2,1)S(1)}, bf16[1536,384]{1,0:T(8,128)(2,1)S(1)}, bf16[256,1536]{1,0:T(8,128)(2,1)S(1)}) custom-call(s32[1]{0:T(128)} %bitcast.core_ref, bf16[1024,384]{1,0:T(8,128)(2,1)} %get-tuple-element.26.half_ref, bf16[1024,384]{1,0:T(8,128)(2,1)} %collective-permute-done.11.other_ref, ...), custom_call_target="tpu_custom_call" | custom-call | flops 402653184 | bytes 12582912 | tf_op jit(solution)/shard_map/project/pallas_call | solution.py:416
  102.5 4.4 %collective-permute-done.12.far_ref = bf16[1024,128]{1,0:T(8,128)(2,1)S(1)} collective-permute-done((bf16[1024,128]{1,0:T(8,128)(2,1)S(1)}, bf16[1024,128]{1,0:T(8,128)(2,1)S(1)}, u32[]{:S(2)}, u32[]{:S(2)}) %collective-permute-start.12) | collective-permute-done | bytes 262176 | tf_op jit(solution)/shard_map/keys/ppermute | solution.py:39
  109.3 22.9 %attention.1 = (bf16[1024,256]{1,0:T(8,128)(2,1)S(1)}, bf16[1024,256]{1,0:T(8,128)(2,1)S(1)}, bf16[2048,128]{1,0:T(8,128)(2,1)S(1)}, bf16[2048,128]{1,0:T(8,128)(2,1)S(1)}) custom-call(s32[1]{0:T(128)} %bitcast.core_ref, bf16[1024,256]{1,0:T(8,128)(2,1)S(1)} %convolution_convert_fusion.1.q_ref, bf16[1024,128]{1,0:T(8,128)(2,1)S(1)} %get-tuple-element.29.near_ref, ...), custom_call_target="tpu_custom_call" | custom-call | flops 5368709120 | bytes 2097152 | tf_op jit(solution)/shard_map/attention/pallas_call | solution.py:141
  138.8 6.1 %projection_gradient.1 = (bf16[4,4,128,384]{3,2,1,0:T(8,128)(2,1)S(1)}, bf16[768,1152]{1,0:T(8,128)(2,1)}) custom-call(s32[1]{0:T(128)S(6)} %add.190.core_ref, bf16[1024,1536]{1,0:T(8,128)(2,1)} %copy-done.2, bf16[1024,256]{1,0:T(8,128)(2,1)S(1)} %get-tuple-element.31.query_ref, bf16[1024,256]{1,0:T(8,128)(2,1)S(1)} %get-tuple-element.39.attended_ref, ...), custom_call_target="tpu_custom_call" | custom-call | flops 1000 | bytes 1000 | tf_op jit(solution)/shard_map/projection_grads/projection_gradient/pallas_call | solution.py:499
  149.9 5.4 %collective-permute-done.18 = bf16[1024,128]{1,0:T(8,128)(2,1)S(1)} collective-permute-done((bf16[1024,128]{1,0:T(8,128)(2,1)S(1)}, bf16[1024,128]{1,0:T(8,128)(2,1)S(1)}, u32[]{:S(2)}, u32[]{:S(2)}) %collective-permute-start.18) | collective-permute-done | bytes 262176 | tf_op jit(solution)/shard_map/key_grads/ppermute | solution.py:39
  155.5 11.2 %collective-permute-start.19 = (bf16[512,128]{1,0:T(8,128)(2,1)S(1)}, bf16[512,128]{1,0:T(8,128)(2,1)S(1)}, u32[]{:S(2)}, u32[]{:S(2)}) collective-permute-start(bf16[512,128]{1,0:T(8,128)(2,1)S(1)} %get-tuple-element.89), channel_id=1, source_target_pairs={{0,1},{1,0},{2,3},{3,2},{4,5},{5,4},{6,7},{7,6},{8,9},{9,8},{10,11... | collective-permute-start | bytes 393224 | tf_op jit(solution)/shard_map/key_grads/ppermute | solution.py:39
  168.4 5.5 %middle_gradient.1 = (f32[512,1536]{1,0:T(8,128)S(1)}, bf16[512,384]{1,0:T(8,128)(2,1)S(1)}, bf16[512,384]{1,0:T(8,128)(2,1)S(1)}, f32[8,1536]{1,0:T(8,128)S(1)}) custom-call(s32[1]{0:T(128)} %bitcast.core_ref, bf16[512,256]{1,0:T(8,128)(2,1)S(1)} %get-tuple-element.58.query_ref, bf16[512,256]{1,0:T(8,128)(2,1)S(1)} %collective-permute-done.16.query_other_ref, ...), custom_call_target="tpu_custom_call" | custom-call | flops 1207959552 | bytes 9437184 | tf_op jit(solution)/shard_map/middle_gradient/pallas_call | solution.py:564
  177.1 5.0 %conv_terms.1 = bf16[4,4,2,6,24,384]{5,4,3,2,1,0:T(8,128)(2,1)S(1)} custom-call(s32[1]{0:T(128)} %bitcast.core_ref, bf16[768,1152]{1,0:T(8,128)(2,1)S(1)} %copy-done.22, bf16[512,384]{1,0:T(8,128)(2,1)S(1)} %get-tuple-element.34.keep_ref, bf16[512,384]{1,0:T(8,128)(2,1)S(1)} %collective-permute-done.24.sent_ref, bf16[2,4,4,24,384]{4,3,2,1,0:T(8,128)(2,1)S(1)} %fusion.14.kv_ref), custom_call_target="tpu_custom_call" | custom-call | flops 3397386240 | bytes 3538944 | tf_op jit(solution)/shard_map/conv_terms/pallas_call | solution.py:624
  186.9 3.6 %collective-permute-start.21 = (bf16[2,768]{1,0:T(2,128)(2,1)S(1)}, bf16[2,768]{1,0:T(2,128)(2,1)S(1)}, u32[]{:S(2)}, u32[]{:S(2)}) collective-permute-start(bf16[2,768]{1,0:T(2,128)(2,1)S(1)} %pad_maximum_fusion.10), channel_id=1, source_target_pairs={{0,1},{1,2},{2,3},{4,5},{5,6},{6,7},{8,9},{9,10},{10,11},{12,13},{... | collective-permute-start | bytes 9224 | tf_op jit(solution)/shard_map/conv_grad/ppermute | solution.py:800
  193.7 11.9 %input_gradient.1 = (bf16[512,1536]{1,0:T(8,128)(2,1)}, f32[8,768]{1,0:T(8,128)S(1)}) custom-call(bf16[512,384]{1,0:T(8,128)(2,1)S(1)} %get-tuple-element.34.keep_ref, bf16[512,384]{1,0:T(8,128)(2,1)S(1)} %copy-done.19, bf16[2,768]{1,0:T(2,128)(2,1)S(1)} %collective-permute-done.21.before_ref, bf16[2,768]{1,0:T(2,128)(2,1)S(1)} %collective-permute-done.22.after_ref, ...), custom_call_target="tpu_custom_call" | custom-call | flops 3019898880 | bytes 12582912 | tf_op jit(solution)/shard_map/input_gradient/pallas_call | solution.py:335
  214.4 2.9 %collective-permute-start.31 = (bf16[128,384]{1,0:T(8,128)(2,1)S(1)}, bf16[128,384]{1,0:T(8,128)(2,1)S(1)}, u32[]{:S(2)}, u32[]{:S(2)}) collective-permute-start(bf16[128,384]{1,0:T(8,128)(2,1)S(1)} %get-tuple-element.62), channel_id=1, source_target_pairs={{0,8},{4,12},{8,0},{12,4},{1,9},{5,13},{9,1},{13,5},{2,10},{6,14},... | collective-permute-start | bytes 294920 | tf_op jit(solution)/shard_map/reduce_all/ppermute | solution.py:35
  220.0 5.6 %reduce-scatter.3.cloned.1.call-done = bf16[1,4,288,384]{3,2,1,0:T(8,128)(2,1)} async-done(((bf16[4,4,288,384]{3,2,1,0:T(8,128)(2,1)}), bf16[1,4,288,384]{3,2,1,0:T(8,128)(2,1)}) %reduce-scatter.3.cloned.1.call-update) | async-done | bytes 884752 | tf_op jit(solution)/shard_map/reduce_conv/reduce_scatter | solution.py:814
  226.9 2.8 %collective-permute-start.28 = (bf16[304,384]{1,0:T(8,128)(2,1)S(1)}, bf16[304,384]{1,0:T(8,128)(2,1)S(1)}, u32[]{:S(2)}, u32[]{:S(2)}) collective-permute-start(bf16[304,384]{1,0:T(8,128)(2,1)S(1)} %get-tuple-element.54), channel_id=1, source_target_pairs={{0,8},{4,12},{8,0},{12,4},{1,9},{5,13},{9,1},{13,5},{2,10},{6,14},... | collective-permute-start | bytes 700424 | tf_op jit(solution)/shard_map/reduce_all/ppermute | solution.py:35
  235.1 6.0 %collective-permute-done.29 = bf16[304,384]{1,0:T(8,128)(2,1)S(1)} collective-permute-done((bf16[304,384]{1,0:T(8,128)(2,1)S(1)}, bf16[304,384]{1,0:T(8,128)(2,1)S(1)}, u32[]{:S(2)}, u32[]{:S(2)}) %collective-permute-start.29) | collective-permute-done | bytes 233504 | tf_op jit(solution)/shard_map/reduce_all/ppermute | solution.py:35
  244.1 4.6 %collective-permute-done.34 = bf16[248,384]{1,0:T(8,128)(2,1)S(1)} collective-permute-done((bf16[248,384]{1,0:T(8,128)(2,1)S(1)}, bf16[248,384]{1,0:T(8,128)(2,1)S(1)}, u32[]{:S(2)}, u32[]{:S(2)}) %collective-permute-start.34) | collective-permute-done | bytes 190496 | tf_op jit(solution)/shard_map/reduce_all/ppermute | solution.py:39
  253.7 5.7 %collective-permute-done.37 = bf16[248,384]{1,0:T(8,128)(2,1)S(1)} collective-permute-done((bf16[248,384]{1,0:T(8,128)(2,1)S(1)}, bf16[248,384]{1,0:T(8,128)(2,1)S(1)}, u32[]{:S(2)}, u32[]{:S(2)}) %collective-permute-start.37) | collective-permute-done | bytes 190496 | tf_op jit(solution)/shard_map/reduce_all/ppermute | solution.py:43
  (228 shorter events, 93.2 us)
Async XLA Ops:
  7.2 73.1 %all-gather.3.cloned.1.call-start = ((), (), s32[]{:S(2)}) async-start(), calls=%async_computation.4 | async-start | bytes 5222400 | tf_op jit(solution)/shard_map/gather/all_gather | solution.py:716
  11.0 7.8 %collective-permute-start.3 = (bf16[48,1920]{1,0:T(8,128)(2,1)}, bf16[48,1920]{1,0:T(8,128)(2,1)}, u32[]{:S(2)}, u32[]{:S(2)}) collective-permute-start(bf16[48,1920]{1,0:T(8,128)(2,1)} %maximum_maximum_fusion), channel_id=1, source_target_pairs={{0,64},{64,0},{1,65},{65,1},{2,66},{66,2},{3,67},{67,3},{4,68},{68... | collective-permute-start | bytes 552968 | tf_op jit(solution)/shard_map/gather/ppermute | solution.py:39
  21.4 191.9 %reduce-scatter.5.cloned.1.call-start = ((), (), s32[]{:S(2)}) async-start(), calls=%async_computation.3 | async-start | bytes 1966080 | tf_op jit(solution)/shard_map/projection_grads/reduce_scatter | solution.py:786
  21.5 28.8 %collective-permute-start = (bf16[512,1536]{1,0:T(8,128)(2,1)S(1)}, bf16[512,1536]{1,0:T(8,128)(2,1)}, u32[]{:S(2)}, u32[]{:S(2)}) collective-permute-start(bf16[512,1536]{1,0:T(8,128)(2,1)S(1)} %bitcast.79), channel_id=1, source_target_pairs={{0,1},{1,0},{2,3},{3,2},{4,5},{5,4},{6,7},{7,6},{8,9},{9,8},{10,11... | collective-permute-start | bytes 4718600 | tf_op jit(solution)/shard_map/rows/ppermute | solution.py:39
  30.5 61.6 %collective-permute-start.15 = (bf16[512,1536]{1,0:T(8,128)(2,1)S(1)}, bf16[512,1536]{1,0:T(8,128)(2,1)}, u32[]{:S(2)}, u32[]{:S(2)}) collective-permute-start(bf16[512,1536]{1,0:T(8,128)(2,1)S(1)} %bitcast.87), channel_id=1, source_target_pairs={{0,1},{1,0},{2,3},{3,2},{4,5},{5,4},{6,7},{7,6},{8,9},{9,8},{10,11... | collective-permute-start | bytes 4718600 | tf_op jit(solution)/shard_map/rows/ppermute | solution.py:39
  36.9 9.2 %collective-permute-start.9 = (bf16[32,72]{1,0:T(8,128)(2,1)S(1)}, bf16[32,72]{1,0:T(8,128)(2,1)S(1)}, u32[]{:S(2)}, u32[]{:S(2)}) collective-permute-start(bf16[32,72]{1,0:T(8,128)(2,1)S(1)} %add_add_fusion.2), channel_id=1, source_target_pairs={{0,32},{16,48},{32,0},{48,16},{1,33},{17,49},{33,1},{49,17},{2,34}... | collective-permute-start | bytes 13832 | tf_op jit(solution)/shard_map/gather_gains/ppermute | solution.py:35
  38.2 10.8 %collective-permute-start.1 = (bf16[2,1536]{1,0:T(2,128)(2,1)S(1)}, bf16[2,1536]{1,0:T(2,128)(2,1)S(1)}, u32[]{:S(2)}, u32[]{:S(2)}) collective-permute-start(bf16[2,1536]{1,0:T(2,128)(2,1)S(1)} %fusion.43), channel_id=1, source_target_pairs={{2,0},{1,3},{6,4},{5,7},{10,8},{9,11},{14,12},{13,15},{18,16},{17,... | collective-permute-start | bytes 18440 | tf_op jit(solution)/shard_map/rows/ppermute | solution.py:721
  41.3 7.7 %collective-permute-start.2 = (bf16[2,1536]{1,0:T(2,128)(2,1)S(1)}, bf16[2,1536]{1,0:T(2,128)(2,1)S(1)}, u32[]{:S(2)}, u32[]{:S(2)}) collective-permute-start(bf16[2,1536]{1,0:T(2,128)(2,1)S(1)} %fusion.43), channel_id=1, source_target_pairs={{2,1},{1,2},{6,5},{5,6},{10,9},{9,10},{14,13},{13,14},{18,17},{17,... | collective-permute-start | bytes 18440 | tf_op jit(solution)/shard_map/rows/ppermute | solution.py:721
  91.9 44.9 %collective-permute-start.23 = (bf16[768,1920]{1,0:T(8,128)(2,1)}, bf16[768,1920]{1,0:T(8,128)(2,1)}, u32[]{:S(2)}, u32[]{:S(2)}) collective-permute-start(bf16[768,1920]{1,0:T(8,128)(2,1)} %get-tuple-element.36.weight_ref), channel_id=1, source_target_pairs={{0,1},{1,0},{2,3},{3,2},{4,5},{5,4},{6,7},{7,6},{8,9},{9,8},{10,11... | collective-permute-start | bytes 8847368 | tf_op jit(solution)/shard_map/projection_grads/ppermute | solution.py:39
  99.4 7.6 %collective-permute-start.12 = (bf16[1024,128]{1,0:T(8,128)(2,1)S(1)}, bf16[1024,128]{1,0:T(8,128)(2,1)S(1)}, u32[]{:S(2)}, u32[]{:S(2)}) collective-permute-start(bf16[1024,128]{1,0:T(8,128)(2,1)S(1)} %get-tuple-element.29.near_ref), channel_id=1, source_target_pairs={{0,2},{2,0},{1,3},{3,1},{4,6},{6,4},{5,7},{7,5},{8,10},{10,8},{9,1... | collective-permute-start | bytes 786440 | tf_op jit(solution)/shard_map/keys/ppermute | solution.py:39
  100.6 8.5 %collective-permute-start.13 = (bf16[1024,128]{1,0:T(8,128)(2,1)S(1)}, bf16[1024,128]{1,0:T(8,128)(2,1)S(1)}, u32[]{:S(2)}, u32[]{:S(2)}) collective-permute-start(bf16[1024,128]{1,0:T(8,128)(2,1)S(1)} %get-tuple-element.29.near_ref), channel_id=1, source_target_pairs={{0,1},{1,0},{2,3},{3,2},{4,5},{5,4},{6,7},{7,6},{8,9},{9,8},{10,11... | collective-permute-start | bytes 786440 | tf_op jit(solution)/shard_map/keys/ppermute | solution.py:39
  101.3 34.4 %collective-permute-start.20 = (bf16[1536,384]{1,0:T(8,128)(2,1)S(1)}, bf16[1536,384]{1,0:T(8,128)(2,1)S(1)}, u32[]{:S(2)}, u32[]{:S(2)}) collective-permute-start(bf16[1536,384]{1,0:T(8,128)(2,1)S(1)} %get-tuple-element.28.weight_ref), channel_id=1, source_target_pairs={{0,1},{1,0},{2,3},{3,2},{4,5},{5,4},{6,7},{7,6},{8,9},{9,8},{10,11... | collective-permute-start | bytes 3538952 | tf_op jit(solution)/shard_map/projection_grads/ppermute | solution.py:39
  146.1 79.5 %reduce-scatter.3.cloned.1.call-start = ((), (), s32[]{:S(2)}) async-start(), calls=%async_computation.2 | async-start | bytes 4423680 | tf_op jit(solution)/shard_map/reduce_conv/reduce_scatter | solution.py:814
  147.7 7.6 %collective-permute-start.18 = (bf16[1024,128]{1,0:T(8,128)(2,1)S(1)}, bf16[1024,128]{1,0:T(8,128)(2,1)S(1)}, u32[]{:S(2)}, u32[]{:S(2)}) collective-permute-start(bf16[1024,128]{1,0:T(8,128)(2,1)S(1)} %slice.376), channel_id=1, source_target_pairs={{0,2},{2,0},{1,3},{3,1},{4,6},{6,4},{5,7},{7,5},{8,10},{10,8},{9,1... | collective-permute-start | bytes 786440 | tf_op jit(solution)/shard_map/key_grads/ppermute | solution.py:39
  149.2 17.7 %collective-permute-start.16 = (bf16[512,256]{1,0:T(8,128)(2,1)S(1)}, bf16[512,256]{1,0:T(8,128)(2,1)S(1)}, u32[]{:S(2)}, u32[]{:S(2)}) collective-permute-start(bf16[512,256]{1,0:T(8,128)(2,1)S(1)} %get-tuple-element.57), channel_id=1, source_target_pairs={{0,1},{1,0},{2,3},{3,2},{4,5},{5,4},{6,7},{7,6},{8,9},{9,8},{10,11... | collective-permute-start | bytes 786440 | tf_op jit(solution)/shard_map/key_grads/ppermute | solution.py:39
  155.5 12.2 %collective-permute-start.19 = (bf16[512,128]{1,0:T(8,128)(2,1)S(1)}, bf16[512,128]{1,0:T(8,128)(2,1)S(1)}, u32[]{:S(2)}, u32[]{:S(2)}) collective-permute-start(bf16[512,128]{1,0:T(8,128)(2,1)S(1)} %get-tuple-element.89), channel_id=1, source_target_pairs={{0,1},{1,0},{2,3},{3,2},{4,5},{5,4},{6,7},{7,6},{8,9},{9,8},{10,11... | collective-permute-start | bytes 393224 | tf_op jit(solution)/shard_map/key_grads/ppermute | solution.py:39
  214.4 15.6 %collective-permute-start.31 = (bf16[128,384]{1,0:T(8,128)(2,1)S(1)}, bf16[128,384]{1,0:T(8,128)(2,1)S(1)}, u32[]{:S(2)}, u32[]{:S(2)}) collective-permute-start(bf16[128,384]{1,0:T(8,128)(2,1)S(1)} %get-tuple-element.62), channel_id=1, source_target_pairs={{0,8},{4,12},{8,0},{12,4},{1,9},{5,13},{9,1},{13,5},{2,10},{6,14},... | collective-permute-start | bytes 294920 | tf_op jit(solution)/shard_map/reduce_all/ppermute | solution.py:35
  217.3 15.1 %collective-permute-start.32 = (bf16[128,384]{1,0:T(8,128)(2,1)S(1)}, bf16[128,384]{1,0:T(8,128)(2,1)S(1)}, u32[]{:S(2)}, u32[]{:S(2)}) collective-permute-start(bf16[128,384]{1,0:T(8,128)(2,1)S(1)} %get-tuple-element.64), channel_id=1, source_target_pairs={{0,4},{4,8},{8,12},{12,0},{1,5},{5,9},{9,13},{13,1},{2,6},{6,10},{... | collective-permute-start | bytes 294920 | tf_op jit(solution)/shard_map/reduce_all/ppermute | solution.py:35
  217.6 14.8 %collective-permute-start.33 = (bf16[128,384]{1,0:T(8,128)(2,1)S(1)}, bf16[128,384]{1,0:T(8,128)(2,1)S(1)}, u32[]{:S(2)}, u32[]{:S(2)}) collective-permute-start(bf16[128,384]{1,0:T(8,128)(2,1)S(1)} %get-tuple-element.63), channel_id=1, source_target_pairs={{0,12},{4,0},{8,4},{12,8},{1,13},{5,1},{9,5},{13,9},{2,14},{6,2},{... | collective-permute-start | bytes 294920 | tf_op jit(solution)/shard_map/reduce_all/ppermute | solution.py:35
  226.9 8.2 %collective-permute-start.28 = (bf16[304,384]{1,0:T(8,128)(2,1)S(1)}, bf16[304,384]{1,0:T(8,128)(2,1)S(1)}, u32[]{:S(2)}, u32[]{:S(2)}) collective-permute-start(bf16[304,384]{1,0:T(8,128)(2,1)S(1)} %get-tuple-element.54), channel_id=1, source_target_pairs={{0,8},{4,12},{8,0},{12,4},{1,9},{5,13},{9,1},{13,5},{2,10},{6,14},... | collective-permute-start | bytes 700424 | tf_op jit(solution)/shard_map/reduce_all/ppermute | solution.py:35
  229.7 11.4 %collective-permute-start.29 = (bf16[304,384]{1,0:T(8,128)(2,1)S(1)}, bf16[304,384]{1,0:T(8,128)(2,1)S(1)}, u32[]{:S(2)}, u32[]{:S(2)}) collective-permute-start(bf16[304,384]{1,0:T(8,128)(2,1)S(1)} %get-tuple-element.55), channel_id=1, source_target_pairs={{0,4},{4,8},{8,12},{12,0},{1,5},{5,9},{9,13},{13,1},{2,6},{6,10},{... | collective-permute-start | bytes 700424 | tf_op jit(solution)/shard_map/reduce_all/ppermute | solution.py:35
  230.0 11.1 %collective-permute-start.30 = (bf16[304,384]{1,0:T(8,128)(2,1)S(1)}, bf16[304,384]{1,0:T(8,128)(2,1)S(1)}, u32[]{:S(2)}, u32[]{:S(2)}) collective-permute-start(bf16[304,384]{1,0:T(8,128)(2,1)S(1)} %get-tuple-element.56), channel_id=1, source_target_pairs={{0,12},{4,0},{8,4},{12,8},{1,13},{5,1},{9,5},{13,9},{2,14},{6,2},{... | collective-permute-start | bytes 700424 | tf_op jit(solution)/shard_map/reduce_all/ppermute | solution.py:35
  241.3 7.4 %collective-permute-start.34 = (bf16[248,384]{1,0:T(8,128)(2,1)S(1)}, bf16[248,384]{1,0:T(8,128)(2,1)S(1)}, u32[]{:S(2)}, u32[]{:S(2)}) collective-permute-start(bf16[248,384]{1,0:T(8,128)(2,1)S(1)} %fusion.32), channel_id=1, source_target_pairs={{0,64},{64,0},{1,65},{65,1},{2,66},{66,2},{3,67},{67,3},{4,68},{68... | collective-permute-start | bytes 571400 | tf_op jit(solution)/shard_map/reduce_all/ppermute | solution.py:39
  251.7 7.7 %collective-permute-start.37 = (bf16[248,384]{1,0:T(8,128)(2,1)S(1)}, bf16[248,384]{1,0:T(8,128)(2,1)S(1)}, u32[]{:S(2)}, u32[]{:S(2)}) collective-permute-start(bf16[248,384]{1,0:T(8,128)(2,1)S(1)} %add_convert_fusion.2), channel_id=1, source_target_pairs={{0,3},{1,2},{2,1},{3,0},{4,7},{5,6},{6,5},{7,4},{8,11},{9,10},{10,... | collective-permute-start | bytes 571400 | tf_op jit(solution)/shard_map/reduce_all/ppermute | solution.py:43
  (49 other events, 232.8 us)
Sparse Core Ops, SparseCore 0:
  21.6 58.6 all-gather.2
  146.2 24.3 reduce-scatter.4
  184.0 41.4 reduce-scatter.2
